TPU v7x, 256 devices: a whole 4x4x8 slice. The times are simulated.
256 devices in a mesh: lat: 8 (over x_lo, y), lon: 32 (over z, x_hi, core).
Axes of the slice: x: 4 (x_hi: 2, x_lo: 2; x = x_hi * 2 + x_lo), y: 4, z: 8, core: 2. Of those that a mesh axis runs over, the one named last changes fastest.
Arguments:
- queries: bfloat16 [128, 512, 768], P('lat', 'lon'), may hold values from -28 to 28
- key_vectors: bfloat16 [128, 512, 768], P('lat', 'lon'), may hold values from -6 to 6
- value_vectors: bfloat16 [128, 512, 768], P('lat', 'lon'), may hold values from -6 to 6
- grad_output: bfloat16 [128, 512, 1536], P('lat', 'lon'), may hold values from -6 to 6
- out_weight: bfloat16 [768, 1536], replicated, may hold values from -0.21875 to 0.21875
Outputs:
- grad_queries: bfloat16 [128, 512, 768], P('lat', 'lon')
- grad_keys: bfloat16 [128, 512, 768], P('lat', 'lon')
- grad_values: bfloat16 [128, 512, 768], P('lat', 'lon')
- grad_weight: float32 [768, 1536], replicated
All inputs are finite; a program needn't handle non-finite values.
Results may differ from a plain program's by a relative error of at most 0.019.
Values may be sent and summed in bfloat16 or wider, within the bound.
No kernel may reach another device: no remote copies, remote signals or barrier semaphores. Data moves between devices by JAX's collectives and lax.ppermute only.
A program may use at most 128 MiB of HBM per device.

v0:
```python
import jax
import jax.numpy as jnp
from jax import lax
from jax.sharding import PartitionSpec as P

HEADS = 6
HEAD_DIM = 128
WIN = 13


def with_halo(cells, sides, width, closed):
    for axis, dim in sides:
        count = lax.axis_size(axis)
        ends = count if closed else count - 1
        head = lax.slice_in_dim(cells, 0, width, axis=dim)
        tail = lax.slice_in_dim(cells, cells.shape[dim] - width, cells.shape[dim], axis=dim)
        cells = jnp.concatenate(
            [
                lax.ppermute(tail, axis, [(i, (i + 1) % count) for i in range(ends)]),
                cells,
                lax.ppermute(head, axis, [((i + 1) % count, i) for i in range(ends)]),
            ],
            axis=dim,
        )
    return cells


def from_behind(shard, axis, by):
    peers = lax.axis_size(axis)
    return lax.ppermute(shard, axis, [(i, (i + by) % peers) for i in range(peers)])


def shifted(block, axis, distance):
    devices = range(lax.axis_size(axis))
    route = [(i - distance, i) for i in devices if i - distance in devices]
    return lax.ppermute(block, axis, route)


def softmax_block(query_tile, key_tile, value_tile, grad_tile, keep_mask, q_scale):
    scores = (
        jnp.einsum("qhd,khd->hqk", query_tile, key_tile, preferred_element_type=jnp.float32)
        * q_scale
    )
    scores = jnp.where(keep_mask[None], scores, -1e30)
    row_max = jnp.max(scores, axis=2, keepdims=True)
    exponent = jnp.exp(scores - row_max)
    row_total = jnp.sum(exponent, axis=2, keepdims=True)
    prob_f = exponent / row_total
    prob_b = prob_f.astype(jnp.bfloat16)
    attended = jnp.einsum(
        "hqk,khd->qhd", prob_b, value_tile, preferred_element_type=jnp.float32
    ).astype(jnp.bfloat16)
    grad_prob = jnp.einsum(
        "qhd,khd->hqk", grad_tile, value_tile, preferred_element_type=jnp.float32
    )
    delta = jnp.sum(prob_f * grad_prob, axis=2, keepdims=True)
    grad_score = (prob_f * (grad_prob - delta) * q_scale).astype(jnp.bfloat16)
    grad_query = jnp.einsum(
        "hqk,khd->qhd", grad_score, key_tile, preferred_element_type=jnp.float32
    ).astype(jnp.bfloat16)
    log_total = row_max + jnp.log(row_total)
    return (attended, grad_query, grad_score, prob_b, log_total[:, :, 0].T, delta[:, :, 0].T)


def local(queries, key_vectors, value_vectors, grad_output, out_weight):
    band_rows, band_cols, channels = queries.shape
    head_count = HEADS
    head_dim = HEAD_DIM
    win_reach = (WIN - 1) // 2
    tile_rows = 8
    q_scale = head_dim ** (-0.5)
    total_rows = band_rows * lax.axis_size("lat")
    first_row = lax.axis_index("lat") * band_rows
    grad_attn = jnp.einsum(
        "tw,cw->tc",
        grad_output.reshape(band_rows * band_cols, -1),
        out_weight,
        preferred_element_type=jnp.float32,
    )
    grad_attn = grad_attn.astype(jnp.bfloat16).reshape(band_rows, band_cols, channels)
    key_value = jnp.concatenate([key_vectors, value_vectors], axis=2)
    cycle_wide = with_halo(key_value, (("lon", 1),), win_reach, True)
    padded = with_halo(cycle_wide, (("lat", 0),), win_reach, False)
    wide_cols = band_cols + 2 * win_reach
    span_rows = tile_rows + 2 * win_reach
    col_gap = jnp.arange(wide_cols)[None, :] - jnp.arange(band_cols)[:, None]
    col_ok = (col_gap >= 0) & (col_gap <= 2 * win_reach)
    attended_parts, query_parts, log_parts, delta_parts = ([], [], [], [])
    grad_kv = jnp.zeros((band_rows + 2 * win_reach, wide_cols, 2 * channels), jnp.float32)
    for tile in range(band_rows // tile_rows):
        low = tile * tile_rows
        query_rows = first_row + low + jnp.arange(tile_rows)
        win_start = jnp.clip(query_rows - win_reach, 0, total_rows - WIN)
        key_rows = first_row + low - win_reach + jnp.arange(span_rows)
        row_ok = (key_rows[None, :] >= win_start[:, None]) & (
            key_rows[None, :] < win_start[:, None] + WIN
        )
        keep_mask = (row_ok[:, None, :, None] & col_ok[None, :, None, :]).reshape(
            tile_rows * band_cols, span_rows * wide_cols
        )
        query_tile = queries[low : low + tile_rows].reshape(-1, head_count, head_dim)
        grad_tile = grad_attn[low : low + tile_rows].reshape(-1, head_count, head_dim)
        region = padded[low : low + span_rows].reshape(
            span_rows * wide_cols, 2, head_count, head_dim
        )
        attended, grad_query, grad_score, prob_b, log_total, delta = softmax_block(
            query_tile, region[:, 0], region[:, 1], grad_tile, keep_mask, q_scale
        )
        attended_parts.append(attended)
        query_parts.append(grad_query)
        log_parts.append(log_total)
        delta_parts.append(delta)
        grad_key = jnp.einsum(
            "hqk,qhd->khd", grad_score, query_tile, preferred_element_type=jnp.float32
        )
        grad_value = jnp.einsum(
            "hqk,qhd->khd", prob_b, grad_tile, preferred_element_type=jnp.float32
        )
        both_grads = jnp.stack([grad_key, grad_value], axis=1).reshape(
            span_rows, wide_cols, 2 * channels
        )
        grad_kv = grad_kv.at[low : low + span_rows].add(both_grads)
    attended_all = jnp.concatenate(attended_parts, axis=0).reshape(band_rows * band_cols, channels)
    grad_queries = jnp.concatenate(query_parts, axis=0).reshape(band_rows, band_cols, channels)
    weight_term = jnp.einsum(
        "tc,tw->cw",
        attended_all,
        grad_output.reshape(band_rows * band_cols, -1),
        preferred_element_type=jnp.float32,
    )
    grad_weight = lax.psum(weight_term, ("lat", "lon"))
    west_part = from_behind(grad_kv[:, :win_reach].astype(jnp.bfloat16), "lon", -1).astype(
        jnp.float32
    )
    east_part = from_behind(
        grad_kv[:, band_cols + win_reach :].astype(jnp.bfloat16), "lon", 1
    ).astype(jnp.float32)
    middle = grad_kv[:, win_reach : band_cols + win_reach]
    middle = middle.at[:, :win_reach].add(east_part)
    middle = middle.at[:, band_cols - win_reach :].add(west_part)
    north_part = shifted(middle[:win_reach].astype(jnp.bfloat16), "lat", -1).astype(jnp.float32)
    south_part = shifted(middle[band_rows + win_reach :].astype(jnp.bfloat16), "lat", 1).astype(
        jnp.float32
    )
    inner = middle[win_reach : band_rows + win_reach]
    inner = inner.at[:win_reach].add(south_part)
    inner = inner.at[band_rows - win_reach :].add(north_part)
    grad_keys = inner[:, :, :channels].astype(jnp.bfloat16)
    grad_values = inner[:, :, channels:].astype(jnp.bfloat16)
    return (grad_queries, grad_keys, grad_values, grad_weight)


def solution(mesh):
    return jax.shard_map(
        local,
        mesh=mesh,
        in_specs=(
            P("lat", "lon", None),
            P("lat", "lon", None),
            P("lat", "lon", None),
            P("lat", "lon", None),
            P(),
        ),
        out_specs=(P("lat", "lon", None), P("lat", "lon", None), P("lat", "lon", None), P()),
        check_vma=False,
    )
```

profile of v0, /device:TPU:3, one launch (start us, length us, event | category | flops | bytes accessed | tf_op | source)
XLA Modules:
  0.0 414.0 jit_solution(5045588565957388455)
XLA Ops:
  17.9 8.2 %collective-permute-done.1 = bf16[16,6,1536]{2,1,0:T(8,128)(2,1)} collective-permute-done((bf16[16,6,1536]{2,1,0:T(8,128)(2,1)}, bf16[16,6,1536]{2,1,0:T(8,128)(2,1)}, u32[]{:S(2)}, u32[]{:S(2)}) %collective-permute-start.1) | collective-permute-done | bytes 294944 | tf_op jit(solution)/shard_map/ppermute | solution.py:21
  31.6 4.2 %collective-permute-start.3 = (bf16[6,28,1536]{2,1,0:T(8,128)(2,1)}, bf16[6,28,1536]{2,1,0:T(8,128)(2,1)S(1)}, u32[]{:S(2)}, u32[]{:S(2)}) collective-permute-start(bf16[6,28,1536]{2,1,0:T(8,128)(2,1)} %get-tuple-element.85), channel_id=1, source_target_pairs={{32,0},{64,32},{96,64},{128,96},{160,128},{192,160},{224,192},{33,... | collective-permute-start | bytes 1548296 | tf_op jit(solution)/shard_map/ppermute | solution.py:21
  42.5 3.3 collective-permute-done.2
  47.7 3.9 pad_maximum_fusion.5
  51.5 3.6 reshape.401
  64.9 3.8 reshape.405
  71.0 3.6 exponential_reduce_fusion
  74.5 3.3 fusion.43
  77.9 3.7 convolution_bitcast_fusion
  81.6 5.1 %fusion.27 = f32[560,1,6,128]{3,0,2,1:T(8,128)} fusion(f32[6,128,560]{1,2,0:T(8,128)} %fusion.48, bf16[128,6,128]{2,1,0:T(8,128)(2,1)S(1)} %copy-done.15, f32[6,128,560]{1,2,0:T(8,128)} %get-tuple-element.101, f32[6,128]{1,0:T(8,128)S(1)} %get-tuple-element.100), kind=kOutput, calls=%fused_computation.32 | convolution fusion | flops 113112368 | bytes 5360640 | tf_op jit(solution)/shard_map/hqk,qhd->khd/dot_general | solution.py:113
  89.0 3.2 copy.48
  92.2 5.0 %add.143 = f32[20,28,1536]{2,1,0:T(8,128)} reshape(f32[560,2,6,128]{3,2,1,0:T(8,128)} %copy.48) | data formatting | bytes 6881280 | tf_op jit(solution)/shard_map/add | solution.py:122
  97.2 4.1 fusion.24
  103.4 3.2 copy.51
  106.7 5.0 %reshape.409 = f32[20,28,1536]{2,1,0:T(8,128)} reshape(f32[560,2,6,128]{3,2,1,0:T(8,128)} %copy.51) | data formatting | bytes 6881280 | tf_op jit(solution)/shard_map/reshape.132
  129.8 4.1 fusion.36
  133.9 4.6 %collective-permute-done.4 = bf16[28,6,1536]{2,0,1:T(8,128)(2,1)S(1)} collective-permute-done((bf16[28,6,1536]{2,0,1:T(8,128)(2,1)}, bf16[28,6,1536]{2,0,1:T(8,128)(2,1)S(1)}, u32[]{:S(2)}, u32[]{:S(2)}) %collective-permute-start.4) | collective-permute-done | bytes 516128 | tf_op jit(solution)/shard_map/ppermute | solution.py:30
  140.7 7.2 %scatter-add.24 = f32[28,16,1536]{2,1,0:T(8,128)} dynamic-update-slice(f32[28,16,1536]{2,1,0:T(8,128)} %slice.254, f32[28,6,1536]{2,1,0:T(8,128)S(1)} %slice_add_fusion.1, s32[]{:T(128)} %constant.180.clone.1, s32[]{:T(128)} %constant.180.clone.1, s32[]{:T(128)} %constant.180.clone.1) | dynamic-update-slice | bytes 2064388 | tf_op jit(solution)/shard_map/scatter-add | solution.py:139
  149.7 6.4 %scatter-add.25 = f32[28,16,1536]{2,1,0:T(8,128)} dynamic-update-slice(f32[28,16,1536]{2,1,0:T(8,128)} %scatter-add.24, f32[28,6,1536]{2,1,0:T(8,128)S(1)} %slice_add_fusion, s32[]{:T(128)} %constant.180.clone.1, s32[]{:T(128)} %constant.190.clone.1, s32[]{:T(128)} %constant.180.clone.1) | dynamic-update-slice | bytes 2064388 | tf_op jit(solution)/shard_map/scatter-add | solution.py:140
  161.3 4.2 %fusion.39 = bf16[128,6,128]{2,0,1:T(8,128)(2,1)S(1)} fusion(f32[6,128,560]{1,2,0:T(8,128)} %copy-done.4, bf16[560,1,6,128]{3,2,1,0:T(8,128)(2,1)S(1)} %copy-done.5, f32[6,128,560]{1,2,0:T(8,128)} %get-tuple-element.99, f32[6,128]{1,0:T(8,128)S(1)} %get-tuple-element.98), kind=kOutput, calls=%fused_computation.43 | convolution fusion | flops 113210672 | bytes 4500480 | tf_op jit(solution)/shard_map/hqk,khd->qhd/dot_general | solution.py:58
  168.6 5.6 %collective-permute-start.7 = (bf16[6,16,1536]{2,1,0:T(8,128)(2,1)S(1)}, bf16[6,16,1536]{2,1,0:T(8,128)(2,1)S(1)}, u32[]{:S(2)}, u32[]{:S(2)}) collective-permute-start(bf16[6,16,1536]{2,1,0:T(8,128)(2,1)S(1)} %get-tuple-element.86), channel_id=1, source_target_pairs={{32,0},{64,32},{96,64},{128,96},{160,128},{192,160},{224,192},{33,... | collective-permute-start | bytes 884744 | tf_op jit(solution)/shard_map/ppermute | solution.py:36
  175.4 4.6 %collective-permute-done.7 = bf16[6,16,1536]{2,1,0:T(8,128)(2,1)S(1)} collective-permute-done((bf16[6,16,1536]{2,1,0:T(8,128)(2,1)S(1)}, bf16[6,16,1536]{2,1,0:T(8,128)(2,1)S(1)}, u32[]{:S(2)}, u32[]{:S(2)}) %collective-permute-start.7) | collective-permute-done | bytes 294944 | tf_op jit(solution)/shard_map/ppermute | solution.py:36
  181.1 221.0 %all-reduce.3.cloned.1.call-done = f32[768,1536]{1,0:T(8,128)} async-done(((f32[768,1536]{1,0:T(8,128)}), f32[768,1536]{1,0:T(8,128)}) %all-reduce.3.cloned.1.call-update) | async-done | bytes 4718608 | tf_op jit(solution)/shard_map/psum | solution.py:131
  402.1 5.0 %copy.150 = f32[768,1536]{1,0:T(8,128)} copy(f32[768,1536]{1,0:T(8,128)} %all-reduce.3.cloned.1.call-done) | data formatting | bytes 9437184
  (106 shorter events, 73.7 us)
Async XLA Ops:
  7.2 5.7 %copy-start = (bf16[768,1536]{1,0:T(8,128)(2,1)S(1)}, bf16[768,1536]{1,0:T(8,128)(2,1)}, u32[]{:S(2)}) copy-start(bf16[768,1536]{1,0:T(8,128)(2,1)} %param.21) | copy-start | bytes 7077892
  7.2 394.9 %all-reduce.3.cloned.1.call-start = ((), (), s32[]{:S(2)}) async-start(), calls=%async_computation | async-start | bytes 9437184 | tf_op jit(solution)/shard_map/psum | solution.py:131
  10.4 7.5 %collective-permute-start = (bf16[16,6,1536]{2,1,0:T(8,128)(2,1)}, bf16[16,6,1536]{2,1,0:T(8,128)(2,1)S(1)}, u32[]{:S(2)}, u32[]{:S(2)}) collective-permute-start(bf16[16,6,1536]{2,1,0:T(8,128)(2,1)} %get-tuple-element.90), channel_id=1, source_target_pairs={{0,1},{1,2},{2,3},{3,4},{4,5},{5,6},{6,7},{7,8},{8,9},{9,10},{10,1... | collective-permute-start | bytes 884744 | tf_op jit(solution)/shard_map/ppermute | solution.py:19
  12.8 13.2 %collective-permute-start.1 = (bf16[16,6,1536]{2,1,0:T(8,128)(2,1)}, bf16[16,6,1536]{2,1,0:T(8,128)(2,1)}, u32[]{:S(2)}, u32[]{:S(2)}) collective-permute-start(bf16[16,6,1536]{2,1,0:T(8,128)(2,1)} %get-tuple-element.91), channel_id=1, source_target_pairs={{1,0},{2,1},{3,2},{4,3},{5,4},{6,5},{7,6},{8,7},{9,8},{10,9},{11,1... | collective-permute-start | bytes 884744 | tf_op jit(solution)/shard_map/ppermute | solution.py:21
  28.4 17.4 %collective-permute-start.2 = (bf16[6,28,1536]{2,1,0:T(8,128)(2,1)}, bf16[6,28,1536]{2,1,0:T(8,128)(2,1)S(1)}, u32[]{:S(2)}, u32[]{:S(2)}) collective-permute-start(bf16[6,28,1536]{2,1,0:T(8,128)(2,1)} %get-tuple-element.84), channel_id=1, source_target_pairs={{0,32},{32,64},{64,96},{96,128},{128,160},{160,192},{192,224},{1,3... | collective-permute-start | bytes 1548296 | tf_op jit(solution)/shard_map/ppermute | solution.py:19
  31.6 16.0 %collective-permute-start.3 = (bf16[6,28,1536]{2,1,0:T(8,128)(2,1)}, bf16[6,28,1536]{2,1,0:T(8,128)(2,1)S(1)}, u32[]{:S(2)}, u32[]{:S(2)}) collective-permute-start(bf16[6,28,1536]{2,1,0:T(8,128)(2,1)} %get-tuple-element.85), channel_id=1, source_target_pairs={{32,0},{64,32},{96,64},{128,96},{160,128},{192,160},{224,192},{33,... | collective-permute-start | bytes 1548296 | tf_op jit(solution)/shard_map/ppermute | solution.py:21
  56.5 1.8 copy-start.6
  56.5 1.8 copy-start.14
  56.5 1.8 copy-start.19
  60.4 2.0 copy-start.12
  70.6 26.6 %copy-start.4 = (f32[6,128,560]{1,2,0:T(8,128)}, f32[6,128,560]{1,2,0:T(8,128)S(1)}, u32[]{:S(2)}) copy-start(f32[6,128,560]{1,2,0:T(8,128)S(1)} %fusion.49) | copy-start | bytes 5160964
  74.5 3.3 copy-start.10
  77.9 3.8 copy-start.15
  111.7 3.3 copy-start.3
  116.0 3.3 copy-start.2
  119.3 2.0 copy-start.16
  119.3 2.0 copy-start.17
  123.2 2.3 copy-start.8
  124.4 14.0 %collective-permute-start.4 = (bf16[28,6,1536]{2,0,1:T(8,128)(2,1)}, bf16[28,6,1536]{2,0,1:T(8,128)(2,1)S(1)}, u32[]{:S(2)}, u32[]{:S(2)}) collective-permute-start(bf16[28,6,1536]{2,0,1:T(8,128)(2,1)} %copy.52), channel_id=1, source_target_pairs={{0,1},{1,2},{2,3},{3,4},{4,5},{5,6},{6,7},{7,8},{8,9},{9,10},{10,1... | collective-permute-start | bytes 1548296 | tf_op jit(solution)/shard_map/ppermute | solution.py:30
  125.6 22.4 %collective-permute-start.5 = (bf16[28,6,1536]{2,0,1:T(8,128)(2,1)S(1)}, bf16[28,6,1536]{2,0,1:T(8,128)(2,1)S(1)}, u32[]{:S(2)}, u32[]{:S(2)}) collective-permute-start(bf16[28,6,1536]{2,0,1:T(8,128)(2,1)S(1)} %copy.54), channel_id=1, source_target_pairs={{0,31},{1,0},{2,1},{3,2},{4,3},{5,4},{6,5},{7,6},{8,7},{9,8},{10,9... | collective-permute-start | bytes 1548296 | tf_op jit(solution)/shard_map/ppermute | solution.py:30
  156.1 5.2 %copy-start.5 = (bf16[560,1,6,128]{3,2,1,0:T(8,128)(2,1)S(1)}, bf16[560,1,6,128]{3,2,1,0:T(8,128)(2,1)}, u32[]{:S(2)}) copy-start(bf16[560,1,6,128]{3,2,1,0:T(8,128)(2,1)} %get-tuple-element.80) | copy-start | bytes 2580484
  158.2 15.9 %collective-permute-start.6 = (bf16[6,16,1536]{2,1,0:T(8,128)(2,1)S(1)}, bf16[6,16,1536]{2,1,0:T(8,128)(2,1)}, u32[]{:S(2)}, u32[]{:S(2)}) collective-permute-start(bf16[6,16,1536]{2,1,0:T(8,128)(2,1)S(1)} %get-tuple-element.87), channel_id=1, source_target_pairs={{0,32},{32,64},{64,96},{96,128},{128,160},{160,192},{192,224},{1,3... | collective-permute-start | bytes 884744 | tf_op jit(solution)/shard_map/ppermute | solution.py:36
  168.6 11.4 %collective-permute-start.7 = (bf16[6,16,1536]{2,1,0:T(8,128)(2,1)S(1)}, bf16[6,16,1536]{2,1,0:T(8,128)(2,1)S(1)}, u32[]{:S(2)}, u32[]{:S(2)}) collective-permute-start(bf16[6,16,1536]{2,1,0:T(8,128)(2,1)S(1)} %get-tuple-element.86), channel_id=1, source_target_pairs={{32,0},{64,32},{96,64},{128,96},{160,128},{192,160},{224,192},{33,... | collective-permute-start | bytes 884744 | tf_op jit(solution)/shard_map/ppermute | solution.py:36
  402.1 5.0 %copy-start.1 = (bf16[768,1536]{1,0:T(8,128)(2,1)S(1)}, bf16[768,1536]{1,0:T(8,128)(2,1)}, u32[]{:S(2)}) copy-start(bf16[768,1536]{1,0:T(8,128)(2,1)} %param.21) | copy-start | bytes 7077892
  (5 other events, 5.8 us)
Sparse Core Ops, SparseCore 0:
  128.7 273.3 all-reduce.2
where the time goes:
time: 417 us; the launch traced here: 414 us
  waiting for transfers between devices  245 us (59%)
  local copies, waits for them, and re-layouts  70.5 us (17%)
  matrix products  41.9 us (10%)
  other arithmetic  22.1 us (5%)
  starting transfers between devices  19.7 us (5%)
  between operations  14.4 us (3%)
    psum x1, waiting for transfers between devices, local(): grad_weight = lax.psum(weight_term, ('lat', 'lon'))  221 us
    ppermute x2, waiting for transfers between devices, with_halo(): lax.ppermute(head, axis, [((i + 1) % count, i) for i in range(ends)])  10 us
    unnamed x42, local copies, waits for them, and re-layouts  9.38 us
    dot_general x2, matrix products, local(): jnp.einsum('hqk,qhd->khd', grad_score, query_tile, preferred_element_type...  9.17 us
    ppermute x2, starting transfers between devices, shifted(): return lax.ppermute(block, axis, route)  8.65 us
  transfers between devices with their start and end apart: 9, of which 7 were waited for; matrix products, arithmetic and copies ran while one was open for 11% of the time, Pallas kernels for 0%

commit v1 on v0

v1 whole, which is shorter than its diff:
```python
import jax
import jax.numpy as jnp
import numpy as np
from jax import lax
from jax.experimental import pallas as pl
from jax.experimental.pallas import tpu as pltpu
from jax.sharding import Mesh, PartitionSpec as P

HEADS = 6
HEAD_DIM = 128
WIDTH = 1536
WIN = 13
REACH = 6
ROWS = 16
COLS = 16
CHANNELS = HEADS * HEAD_DIM
TOKENS = ROWS * COLS
EDGE = REACH * COLS
SPAN = ROWS + 2 * REACH
MID = SPAN * COLS
SIDE = SPAN * REACH
SIDE_PAD = 176
TILES = 2
TILE_Q = TOKENS // TILES
MID_TILE = 320
SIDE_TILE = 128
KEYS = MID_TILE + 2 * SIDE_TILE
MID_STARTS = (0, 128)
SIDE_STARTS = (0, 48)
SCALE = HEAD_DIM ** -0.5
LAT = ("xl", "y")
LON = ("z", "xh", "core")
PLANE = ("xl", "y", "xh")
F32 = jnp.float32
BF16 = jnp.bfloat16


def key_places():
    mid_rows, mid_cols = np.divmod(np.arange(MID), COLS)
    side_rows, side_cols = np.divmod(np.arange(SIDE_PAD), REACH)
    unused = np.arange(SIDE_PAD) >= SIDE
    west_cols = np.where(unused, 1000, side_cols - REACH)
    east_cols = np.where(unused, 1000, side_cols + COLS)
    rows, cols = [], []
    for mid, side in zip(MID_STARTS, SIDE_STARTS):
        mids, sides = slice(mid, mid + MID_TILE), slice(side, side + SIDE_TILE)
        rows.append(np.concatenate([mid_rows[mids], side_rows[sides], side_rows[sides]]) - REACH)
        cols.append(np.concatenate([mid_cols[mids], west_cols[sides], east_cols[sides]]))
    return np.stack(rows), np.stack(cols)


def window_bias(first_row, total_rows):
    rows, cols = key_places()
    query_rows, query_cols = np.divmod(np.arange(TOKENS).reshape(TILES, TILE_Q), COLS)
    start = jnp.clip(first_row + query_rows - REACH, 0, total_rows - WIN)[:, None, :]
    key_rows = (first_row + rows)[:, :, None]
    near = np.abs(cols[:, :, None] - query_cols[:, None, :]) <= REACH
    keep = (key_rows >= start) & (key_rows < start + WIN) & near
    return jnp.where(keep, 0.0, -1e30).astype(F32)


def tile_keys(tile, own, edges, west, east):
    side = slice(SIDE_STARTS[tile], SIDE_STARTS[tile] + SIDE_TILE)
    if tile == 0:
        mid = [edges[0], own[: MID_TILE - EDGE]]
    else:
        mid = [own[TOKENS - (MID_TILE - EDGE) :], edges[1]]
    return jnp.concatenate(mid + [west[side], east[side]], axis=0)


def dot(a, b, dims):
    return lax.dot_general(a, b, (dims, ((), ())), preferred_element_type=F32)


def forward_kernel(q_ref, k_ref, v_ref, north_ref, south_ref, west_ref, east_ref, bias_ref, out_ref, lse_ref):
    keys = (k_ref[...], (north_ref[0], south_ref[0]), west_ref[0], east_ref[0])
    values = (v_ref[...], (north_ref[1], south_ref[1]), west_ref[1], east_ref[1])
    for tile in range(TILES):
        span = slice(tile * TILE_Q, (tile + 1) * TILE_Q)
        scores = dot(tile_keys(tile, *keys), q_ref[span, :], ((1,), (1,))) * SCALE + bias_ref[tile]
        top = jnp.max(scores, axis=0, keepdims=True)
        exponent = jnp.exp(scores - top)
        total = jnp.sum(exponent, axis=0, keepdims=True)
        prob = (exponent * (1.0 / total)).astype(BF16)
        attended = dot(prob, tile_keys(tile, *values), ((0,), (0,)))
        out_ref[span, :] = attended.astype(BF16)
        lse_ref[0, tile : tile + 1, :] = top + jnp.log(total)


def backward_kernel(
    q_ref, k_ref, v_ref, north_ref, south_ref, west_ref, east_ref, bias_ref, g_ref, lse_ref,
    dq_ref, mid_ref, dwest_ref, deast_ref, prob_s, score_s,
):
    @pl.when(pl.program_id(0) == 0)
    def _():
        prob_s[...] = jnp.zeros_like(prob_s)
        score_s[...] = jnp.zeros_like(score_s)

    keys = (k_ref[...], (north_ref[0], south_ref[0]), west_ref[0], east_ref[0])
    values = (v_ref[...], (north_ref[1], south_ref[1]), west_ref[1], east_ref[1])
    for tile in range(TILES):
        span = slice(tile * TILE_Q, (tile + 1) * TILE_Q)
        key_tile = tile_keys(tile, *keys)
        scores = dot(key_tile, q_ref[span, :], ((1,), (1,))) * SCALE + bias_ref[tile]
        prob = jnp.exp(scores - lse_ref[0, tile : tile + 1, :])
        grad_prob = dot(tile_keys(tile, *values), g_ref[span, :], ((1,), (1,)))
        delta = jnp.sum(prob * grad_prob, axis=0, keepdims=True)
        grad_score = (prob * (grad_prob - delta) * SCALE).astype(BF16)
        dq_ref[span, :] = dot(grad_score, key_tile, ((0,), (0,))).astype(BF16)
        mid, side = MID_STARTS[tile], SIDE_STARTS[tile]
        for part, scratch in ((prob.astype(BF16), prob_s), (grad_score, score_s)):
            scratch[mid : mid + MID_TILE, span] = part[:MID_TILE]
            for at, low in ((MID, MID_TILE), (MID + SIDE_PAD, MID_TILE + SIDE_TILE)):
                scratch[at + side : at + side + SIDE_TILE, span] = part[low : low + SIDE_TILE]
    for slot, scratch, other in ((0, score_s, q_ref), (1, prob_s, g_ref)):
        grads = dot(scratch[...], other[...], ((1,), (0,)))
        mid_ref[slot] = grads[:MID]
        dwest_ref[slot] = grads[MID : MID + SIDE_PAD].astype(BF16)
        deast_ref[slot] = grads[MID + SIDE_PAD :].astype(BF16)


def head_specs():
    tokens = pl.BlockSpec((TOKENS, HEAD_DIM), lambda h: (0, h))
    edge = pl.BlockSpec((2, EDGE, HEAD_DIM), lambda h: (0, 0, h))
    side = pl.BlockSpec((2, SIDE_PAD, HEAD_DIM), lambda h: (0, 0, h))
    bias = pl.BlockSpec((TILES, KEYS, TILE_Q), lambda h: (0, 0, 0))
    lse = pl.BlockSpec((1, 8, TILE_Q), lambda h: (h, 0, 0))
    mid = pl.BlockSpec((2, MID, HEAD_DIM), lambda h: (0, 0, h))
    return tokens, edge, side, bias, lse, mid


def forward_attention(q, k, v, halos, bias):
    tokens, edge, side, bias_spec, lse, _ = head_specs()
    return pl.pallas_call(
        forward_kernel,
        grid=(HEADS,),
        in_specs=[tokens, tokens, tokens, edge, edge, side, side, bias_spec],
        out_specs=[tokens, lse],
        out_shape=[
            jax.ShapeDtypeStruct((TOKENS, CHANNELS), BF16),
            jax.ShapeDtypeStruct((HEADS, 8, TILE_Q), F32),
        ],
        compiler_params=pltpu.CompilerParams(vmem_limit_bytes=32 * 1024 * 1024),
        cost_estimate=pl.CostEstimate(flops=2 * 10**9, bytes_accessed=8 * 10**6, transcendentals=10**6),
    )(q, k, v, *halos, bias)


def backward_attention(q, k, v, halos, bias, g, lse_array):
    tokens, edge, side, bias_spec, lse, mid = head_specs()
    keys = MID + 2 * SIDE_PAD
    return pl.pallas_call(
        backward_kernel,
        grid=(HEADS,),
        in_specs=[tokens, tokens, tokens, edge, edge, side, side, bias_spec, tokens, lse],
        out_specs=[tokens, mid, side, side],
        out_shape=[
            jax.ShapeDtypeStruct((TOKENS, CHANNELS), BF16),
            jax.ShapeDtypeStruct((2, MID, CHANNELS), F32),
            jax.ShapeDtypeStruct((2, SIDE_PAD, CHANNELS), BF16),
            jax.ShapeDtypeStruct((2, SIDE_PAD, CHANNELS), BF16),
        ],
        scratch_shapes=[pltpu.VMEM((keys, TOKENS), BF16), pltpu.VMEM((keys, TOKENS), BF16)],
        compiler_params=pltpu.CompilerParams(vmem_limit_bytes=32 * 1024 * 1024),
        cost_estimate=pl.CostEstimate(flops=4 * 10**9, bytes_accessed=12 * 10**6, transcendentals=10**6),
    )(q, k, v, *halos, bias, g, lse_array)


def along_lat(block, by):
    count = lax.axis_size(LAT)
    return lax.ppermute(block, LAT, [(i, i + by) for i in range(count) if 0 <= i + by < count])


def along_lon(block, by):
    count = lax.axis_size(LON)
    return lax.ppermute(block, LON, [(i, (i + by) % count) for i in range(count)])


def swapped(block, axis, bit):
    return lax.ppermute(block, axis, [(i, i ^ bit) for i in range(lax.axis_size(axis))])


def strip(keys, values, rows, cols):
    return jnp.stack([keys[rows, cols], values[rows, cols]]).reshape(2, -1, CHANNELS)


def halos_of(keys, values):
    every, first, last = slice(None), slice(0, REACH), slice(ROWS - REACH, ROWS)
    north = along_lat(strip(keys, values, last, every), 1)
    south = along_lat(strip(keys, values, first, every), -1)
    west = along_lon(strip(keys, values, every, last), 1)
    east = along_lon(strip(keys, values, every, first), -1)
    poles = jnp.stack([north, south], axis=1).reshape(2, 2, REACH, COLS, CHANNELS)
    corner_west = along_lon(poles[:, :, :, COLS - REACH :].reshape(2, 2, -1, CHANNELS), 1)
    corner_east = along_lon(poles[:, :, :, :REACH].reshape(2, 2, -1, CHANNELS), -1)
    unused = jnp.zeros((2, SIDE_PAD - SIDE, CHANNELS), BF16)
    west = jnp.concatenate([corner_west[:, 0], west, corner_west[:, 1], unused], axis=1)
    east = jnp.concatenate([corner_east[:, 0], east, corner_east[:, 1], unused], axis=1)
    return north, south, west, east


def sum_of_weight_terms(attended, grad_rows):
    half = CHANNELS // 2
    core = lax.axis_index("core")

    def term(which):
        part = lax.dynamic_slice_in_dim(attended, which * half, half, axis=1)
        return dot(part, grad_rows, ((0,), (0,)))

    received = swapped(term(1 - core).astype(BF16), "core", 1)
    pair = (term(core) + received.astype(F32)).astype(BF16)
    group = lax.axis_size(PLANE)
    pieces = lax.all_to_all(
        pair.reshape(group, half // group, WIDTH), PLANE, split_axis=0, concat_axis=0, tiled=True
    )
    total = jnp.sum(pieces.astype(F32), axis=0)
    for bit in (1, 2, 4):
        mine = total.astype(BF16)
        total = mine.astype(F32) + swapped(mine, "z", bit).astype(F32)
    whole = lax.all_to_all(
        jnp.broadcast_to(total.astype(BF16)[None], (group, half // group, WIDTH)),
        PLANE, split_axis=0, concat_axis=0, tiled=True,
    ).reshape(half, WIDTH)
    other = swapped(whole, "core", 1)
    first = jnp.where(core == 0, whole, other)
    second = jnp.where(core == 0, other, whole)
    return jnp.concatenate([first, second], axis=0).astype(F32)


def local(queries, key_vectors, value_vectors, grad_output, out_weight):
    first_row = lax.axis_index(LAT) * ROWS
    halos = halos_of(key_vectors, value_vectors)
    bias = window_bias(first_row, ROWS * lax.axis_size(LAT))
    grad_rows = grad_output.reshape(TOKENS, WIDTH)
    grad_attn = dot(grad_rows, out_weight, ((1,), (1,))).astype(BF16)
    q = queries.reshape(TOKENS, CHANNELS)
    k = key_vectors.reshape(TOKENS, CHANNELS)
    v = value_vectors.reshape(TOKENS, CHANNELS)
    attended, lse = forward_attention(q, k, v, halos, bias)
    grad_weight = sum_of_weight_terms(attended, grad_rows)
    grad_q, mid, side_west, side_east = backward_attention(q, k, v, halos, bias, grad_attn, lse)

    from_east = along_lon(side_west, -1)[:, :SIDE].reshape(2, SPAN, REACH, CHANNELS).astype(F32)
    from_west = along_lon(side_east, 1)[:, :SIDE].reshape(2, SPAN, REACH, CHANNELS).astype(F32)
    none = jnp.zeros((), F32)
    wide = COLS - REACH
    mid = mid.reshape(2, SPAN, COLS, CHANNELS)
    mid = mid + lax.pad(from_west, none, [(0, 0, 0), (0, 0, 0), (0, wide, 0), (0, 0, 0)])
    mid = mid + lax.pad(from_east, none, [(0, 0, 0), (0, 0, 0), (wide, 0, 0), (0, 0, 0)])
    from_south = along_lat(mid[:, :REACH].astype(BF16), -1).astype(F32)
    from_north = along_lat(mid[:, SPAN - REACH :].astype(BF16), 1).astype(F32)
    inner = mid[:, REACH : SPAN - REACH]
    tall = ROWS - REACH
    inner = inner + lax.pad(from_north, none, [(0, 0, 0), (0, tall, 0), (0, 0, 0), (0, 0, 0)])
    inner = inner + lax.pad(from_south, none, [(0, 0, 0), (tall, 0, 0), (0, 0, 0), (0, 0, 0)])
    inner = inner.astype(BF16)
    return grad_q.reshape(queries.shape), inner[0], inner[1], grad_weight


def solution(mesh):
    fine = Mesh(mesh.devices.reshape(2, 4, 8, 2, 2), LAT + LON)
    spread = P(LAT, LON, None)
    return jax.shard_map(
        local,
        mesh=fine,
        in_specs=(spread, spread, spread, spread, P()),
        out_specs=(spread, spread, spread, P()),
        check_vma=False,
    )
```

time: 417 us -> 158 us (0.38)
  waiting for transfers between devices: 245 us -> 30.1 us
  local copies, waits for them, and re-layouts: 70.5 us -> 22.7 us
  matrix products: 41.9 us -> 5.59 us
  starting transfers between devices: 19.7 us -> 42.6 us
  blocking collectives: 0 us -> 20.3 us
  Pallas kernels: 0 us -> 14.8 us
  between operations: 14.4 us -> 1.15 us
    psum x1 -> x0, waiting for transfers between devices: 221 us -> none  [local(): grad_weight = lax.psum(weight_term, ('lat', 'lon'))]
    dot_general x12 -> x3, matrix products: 36.3 us -> 5.59 us  [dot(): return lax.dot_general(a, b, (dims, ((), ())), preferred_element_type=F32)]
    all_to_all x0 -> x1, blocking collectives: none -> 20.3 us  [sum_of_weight_terms(): lax.all_to_all(pair.reshape(group, half // group, WIDTH), PLANE, split_ax...]
    ppermute x8 -> x15, starting transfers between devices: 19.6 us -> 37.7 us  [the longest x6 13.3 us: along_lon(): lax.ppermute(block, LON, [(i, (i + by) % count) for i in range(count)])]
    scatter-add x3 -> x0, local copies, waits for them, and re-layouts: 16.4 us -> none  [the longest x1 7.23 us: local(): middle = middle.at[:, :win_reach].add(east_part)]
    pallas_call x0 -> x2, Pallas kernels: none -> 14.8 us  [the longest x1 8.88 us: backward_attention(): pl.pallas_call(backward_kernel, grid=(HEADS,), in_specs=[tokens, tokens,...]
    reshape x5 -> x2, local copies, waits for them, and re-layouts: 10.5 us -> 0.06 us  [the longest x1 0.03 us: halos_of(): poles[:, :, :, :REACH].reshape(2, 2, -1, CHANNELS)]
    ppermute x8 -> x15, waiting for transfers between devices: 24.4 us -> 30.1 us  [the longest x6 15.9 us: along_lon(): lax.ppermute(block, LON, [(i, (i + by) % count) for i in range(count)])]
  transfers between devices with their start and end apart: 9 -> 16, of which waited for: 7 -> 8; matrix products, arithmetic and copies ran while one was open for 11% -> 20% of each run, Pallas kernels for 0% -> 6%
where the time goes in v1:
time: 158 us; the launch traced here: 157 us
  starting transfers between devices  42.6 us (27%)
  waiting for transfers between devices  30.1 us (19%)
  local copies, waits for them, and re-layouts  22.7 us (14%)
  blocking collectives  20.3 us (13%)
  other arithmetic  19.4 us (12%)
  Pallas kernels  14.8 us (9%)
  matrix products  5.59 us (4%)
    all_to_all x1, blocking collectives, sum_of_weight_terms(): lax.all_to_all(pair.reshape(group, half // group, WIDTH), PLANE, split_ax...  20.3 us
    ppermute x6, waiting for transfers between devices, along_lon(): lax.ppermute(block, LON, [(i, (i + by) % count) for i in range(count)])  15.9 us
    ppermute x6, starting transfers between devices, along_lon(): lax.ppermute(block, LON, [(i, (i + by) % count) for i in range(count)])  13.3 us
    ppermute x4, starting transfers between devices, along_lat(): lax.ppermute(block, LAT, [(i, i + by) for i in range(count) if 0 <= i + b...  12.6 us
    ppermute x5, starting transfers between devices, swapped(): lax.ppermute(block, axis, [(i, i ^ bit) for i in range(lax.axis_size(axis...  11.7 us
    pallas_call x1, Pallas kernels, backward_attention(): pl.pallas_call(backward_kernel, grid=(HEADS,), in_specs=[tokens, tokens,...  8.88 us
    ppermute x5, waiting for transfers between devices, swapped(): lax.ppermute(block, axis, [(i, i ^ bit) for i in range(lax.axis_size(axis...  8.53 us
    another operation x4, local copies, waits for them, and re-layouts, strip(): jnp.stack([keys[rows, cols], values[rows, cols]]).reshape(2, -1, CHANNELS)  6.57 us
  transfers between devices with their start and end apart: 16, of which 8 were waited for; matrix products, arithmetic and copies ran while one was open for 20% of the time, Pallas kernels for 6%

profile of v1, /device:TPU:3, one launch (start us, length us, event | category | flops | bytes accessed | tf_op | source)
XLA Modules:
  0.0 156.6 jit_solution(230697798457616519)
XLA Ops:
  3.6 3.2 %collective-permute-start = (bf16[2,96,768]{2,1,0:T(8,128)(2,1)}, bf16[2,96,768]{2,1,0:T(8,128)(2,1)S(1)}, u32[]{:S(2)}, u32[]{:S(2)}) collective-permute-start(bf16[2,96,768]{2,1,0:T(8,128)(2,1)} %pad_maximum_fusion), channel_id=1, source_target_pairs={{0,32},{32,64},{64,96},{96,128},{128,160},{160,192},{192,224},{1,3... | collective-permute-start | bytes 884744 | tf_op jit(solution)/shard_map/ppermute | solution.py:170
  7.6 4.2 %collective-permute-start.1 = (bf16[2,96,768]{2,1,0:T(8,128)(2,1)}, bf16[2,96,768]{2,1,0:T(8,128)(2,1)}, u32[]{:S(2)}, u32[]{:S(2)}) collective-permute-start(bf16[2,96,768]{2,1,0:T(8,128)(2,1)} %pad_maximum_fusion.1), channel_id=1, source_target_pairs={{32,0},{64,32},{96,64},{128,96},{160,128},{192,160},{224,192},{33,... | collective-permute-start | bytes 884744 | tf_op jit(solution)/shard_map/ppermute | solution.py:170
  24.6 2.0 %collective-permute-start.3 = (bf16[2,96,768]{2,1,0:T(8,128)(2,1)}, bf16[2,96,768]{2,1,0:T(8,128)(2,1)}, u32[]{:S(2)}, u32[]{:S(2)}) collective-permute-start(bf16[2,96,768]{2,1,0:T(8,128)(2,1)} %pad_maximum_fusion.2), channel_id=1, source_target_pairs={{0,1},{1,2},{2,3},{3,4},{4,5},{5,6},{6,7},{7,8},{8,9},{9,10},{10,1... | collective-permute-start | bytes 884744 | tf_op jit(solution)/shard_map/ppermute | solution.py:175
  29.8 4.4 %collective-permute-start.4 = (bf16[2,2,36,768]{3,2,0,1:T(8,128)(2,1)S(1)}, bf16[2,2,36,768]{3,2,0,1:T(8,128)(2,1)S(1)}, u32[]{:S(2)}, u32[]{:S(2)}) collective-permute-start(bf16[2,2,36,768]{3,2,0,1:T(8,128)(2,1)S(1)} %copy.22), channel_id=1, source_target_pairs={{0,31},{1,0},{2,1},{3,2},{4,3},{5,4},{6,5},{7,6},{8,7},{9,8},{10,9... | collective-permute-start | bytes 663560 | tf_op jit(solution)/shard_map/ppermute | solution.py:175
  34.5 2.5 %collective-permute-done.4 = bf16[2,2,36,768]{3,2,0,1:T(8,128)(2,1)S(1)} collective-permute-done((bf16[2,2,36,768]{3,2,0,1:T(8,128)(2,1)S(1)}, bf16[2,2,36,768]{3,2,0,1:T(8,128)(2,1)S(1)}, u32[]{:S(2)}, u32[]{:S(2)}) %collective-permute-start.4) | collective-permute-done | bytes 221216 | tf_op jit(solution)/shard_map/ppermute | solution.py:175
  37.1 3.8 %collective-permute-done.2 = bf16[2,2,36,768]{3,2,0,1:T(8,128)(2,1)S(1)} collective-permute-done((bf16[2,2,36,768]{3,2,0,1:T(8,128)(2,1)S(1)}, bf16[2,2,36,768]{3,2,0,1:T(8,128)(2,1)S(1)}, u32[]{:S(2)}, u32[]{:S(2)}) %collective-permute-start.2) | collective-permute-done | bytes 221216 | tf_op jit(solution)/shard_map/ppermute | solution.py:175
  42.4 6.0 %shard_map.111 = (bf16[256,768]{1,0:T(8,128)(2,1)S(1)}, f32[6,8,128]{2,1,0:T(8,128)S(1)}) custom-call(bf16[256,768]{1,0:T(8,128)(2,1)S(1)} %bitcast.42, bf16[256,768]{1,0:T(8,128)(2,1)S(1)} %bitcast.37, bf16[256,768]{1,0:T(8,128)(2,1)S(1)} %bitcast.39, bf16[2,96,768]{2,1,0:T(8,128)(2,1)S(1)} %copy-done.12, ...), custom_call_target="tpu_custom_call" | custom-call | flops 2000000000 | bytes 8000000 | tf_op jit(solution)/shard_map/pallas_call | solution.py:134
  50.5 8.2 %collective-permute-start.10 = (bf16[384,1536]{1,0:T(8,128)(2,1)}, bf16[384,1536]{1,0:T(8,128)(2,1)}, u32[]{:S(2)}, u32[]{:S(2)}) collective-permute-start(bf16[384,1536]{1,0:T(8,128)(2,1)} %convolution_convert_fusion), channel_id=1, source_target_pairs={{0,1},{1,0},{2,3},{3,2},{4,5},{5,4},{6,7},{7,6},{8,9},{9,8},{10,11... | collective-permute-start | bytes 3538952 | tf_op jit(solution)/shard_map/ppermute | solution.py:179
  58.8 2.8 %collective-permute-done.10 = bf16[384,1536]{1,0:T(8,128)(2,1)} collective-permute-done((bf16[384,1536]{1,0:T(8,128)(2,1)}, bf16[384,1536]{1,0:T(8,128)(2,1)}, u32[]{:S(2)}, u32[]{:S(2)}) %collective-permute-start.10) | collective-permute-done | bytes 1179680 | tf_op jit(solution)/shard_map/ppermute | solution.py:179
  61.6 2.0 %fusion = bf16[384,1536]{1,0:T(8,128)(2,1)S(1)} fusion(bf16[256,1536]{1,0:T(8,128)(2,1)} %bitcast.45, bf16[384,1536]{1,0:T(8,128)(2,1)} %collective-permute-done.10, bf16[256,768]{1,0:T(8,128)(2,1)S(1)} %get-tuple-element.15, s32[]{:T(128)S(6)} %select_n.24), kind=kOutput, calls=%fused_computation.1 | convolution fusion | flops 303759360 | bytes 3342340 | tf_op jit(solution)/shard_map/dot_general | solution.py:72
  63.6 20.3 %all_to_all.10 = bf16[16,24,1536]{2,1,0:T(8,128)(2,1)} all-to-all(bf16[16,24,1536]{2,1,0:T(8,128)(2,1)S(1)} %bitcast.44), channel_id=1, replica_groups=mesh['xl'=2,'y'=4,'z'=8,'xh'=2,'core'=2] {'xl','y','xh'}, dimensions={0} | all-to-all | bytes 2359296 | tf_op jit(solution)/shard_map/all_to_all | solution.py:212
  85.4 3.2 %collective-permute-done.11 = bf16[24,1536]{1,0:T(8,128)(2,1)S(1)} collective-permute-done((bf16[24,1536]{1,0:T(8,128)(2,1)S(1)}, bf16[24,1536]{1,0:T(8,128)(2,1)S(1)}, u32[]{:S(2)}, u32[]{:S(2)}) %collective-permute-start.11) | collective-permute-done | bytes 73760 | tf_op jit(solution)/shard_map/ppermute | solution.py:179
  88.8 2.1 %convolution_convert_fusion.1.g_ref = bf16[256,768]{1,0:T(8,128)(2,1)S(1)} fusion(bf16[256,1536]{1,0:T(8,128)(2,1)} %bitcast.46, bf16[768,1536]{1,0:T(8,128)(2,1)S(1)} %copy-done), kind=kOutput, calls=%fused_computation.9 | convolution fusion | flops 604176384 | bytes 3538944 | tf_op jit(solution)/shard_map/dot_general | solution.py:72
  90.9 2.5 %collective-permute-done.12 = bf16[24,1536]{1,0:T(8,128)(2,1)S(1)} collective-permute-done((bf16[24,1536]{1,0:T(8,128)(2,1)S(1)}, bf16[24,1536]{1,0:T(8,128)(2,1)S(1)}, u32[]{:S(2)}, u32[]{:S(2)}) %collective-permute-start.12) | collective-permute-done | bytes 73760 | tf_op jit(solution)/shard_map/ppermute | solution.py:179
  95.0 8.9 %shard_map.112 = (bf16[256,768]{1,0:T(8,128)(2,1)}, f32[2,448,768]{2,1,0:T(8,128)S(1)}, bf16[2,176,768]{2,1,0:T(8,128)(2,1)}, bf16[2,176,768]{2,1,0:T(8,128)(2,1)}) custom-call(bf16[256,768]{1,0:T(8,128)(2,1)S(1)} %bitcast.43, bf16[256,768]{1,0:T(8,128)(2,1)S(1)} %bitcast.38, bf16[256,768]{1,0:T(8,128)(2,1)S(1)} %bitcast.40, ...), custom_call_target="tpu_custom_call" | custom-call | flops 4000000000 | bytes 12000000 | tf_op jit(solution)/shard_map/pallas_call | solution.py:151
  105.4 4.5 %collective-permute-start.7 = (bf16[2,176,768]{2,1,0:T(8,128)(2,1)}, bf16[2,176,768]{2,1,0:T(8,128)(2,1)S(1)}, u32[]{:S(2)}, u32[]{:S(2)}) collective-permute-start(bf16[2,176,768]{2,1,0:T(8,128)(2,1)} %get-tuple-element.14), channel_id=1, source_target_pairs={{0,31},{1,0},{2,1},{3,2},{4,3},{5,4},{6,5},{7,6},{8,7},{9,8},{10,9... | collective-permute-start | bytes 1622024 | tf_op jit(solution)/shard_map/ppermute | solution.py:175
  112.2 4.9 %all-to-all-start.1 = ((bf16[16,24,1536]{2,1,0:T(8,128)(2,1)}), bf16[16,24,1536]{2,1,0:T(8,128)(2,1)}, u32[]{:S(2)}, u32[]{:S(2)}) async-start(bf16[16,24,1536]{2,1,0:T(8,128)(2,1)} %broadcast_in_dim.22), calls=%async_computation.1 | async-start | bytes 2359296 | tf_op jit(solution)/shard_map/all_to_all | solution.py:219
  117.1 9.6 %collective-permute-done.7 = bf16[2,176,768]{2,1,0:T(8,128)(2,1)S(1)} collective-permute-done((bf16[2,176,768]{2,1,0:T(8,128)(2,1)}, bf16[2,176,768]{2,1,0:T(8,128)(2,1)S(1)}, u32[]{:S(2)}, u32[]{:S(2)}) %collective-permute-start.7) | collective-permute-done | bytes 540704 | tf_op jit(solution)/shard_map/ppermute | solution.py:175
  128.9 3.7 %fusion.8 = (bf16[2,28,16,768]{3,0,2,1:T(2,128)(2,1)S(1)}, f32[2,28,16,768]{3,0,2,1:T(2,128)}) fusion(bf16[2,28,6,768]{3,0,2,1:T(2,128)(2,1)S(1)} %bitcast.48, bf16[2,28,6,768]{3,0,2,1:T(2,128)(2,1)S(1)} %bitcast.49, f32[2,28,16,768]{3,2,1,0:T(8,128)S(1)} %bitcast.36), kind=kLoop, calls=%fused_computation.37 | loop fusion | flops 3440640 | bytes 7913472 | tf_op jit(solution)/shard_map/convert.12
  133.8 2.5 %collective-permute-start.9 = (bf16[2,6,16,768]{3,0,2,1:T(2,128)(2,1)}, bf16[2,6,16,768]{3,0,2,1:T(2,128)(2,1)S(1)}, u32[]{:S(2)}, u32[]{:S(2)}) collective-permute-start(bf16[2,6,16,768]{3,0,2,1:T(2,128)(2,1)} %get-tuple-element.21), channel_id=1, source_target_pairs={{32,0},{64,32},{96,64},{128,96},{160,128},{192,160},{224,192},{33,... | collective-permute-start | bytes 884744 | tf_op jit(solution)/shard_map/ppermute | solution.py:170
  136.3 2.7 %collective-permute-start.8 = (bf16[2,6,16,768]{3,0,2,1:T(2,128)(2,1)S(1)}, bf16[2,6,16,768]{3,0,2,1:T(2,128)(2,1)S(1)}, u32[]{:S(2)}, u32[]{:S(2)}) collective-permute-start(bf16[2,6,16,768]{3,0,2,1:T(2,128)(2,1)S(1)} %get-tuple-element.20), channel_id=1, source_target_pairs={{0,32},{32,64},{64,96},{96,128},{128,160},{160,192},{192,224},{1,3... | collective-permute-start | bytes 884744 | tf_op jit(solution)/shard_map/ppermute | solution.py:170
  142.3 4.1 %collective-permute-done.8 = bf16[2,6,16,768]{3,0,2,1:T(2,128)(2,1)S(1)} collective-permute-done((bf16[2,6,16,768]{3,0,2,1:T(2,128)(2,1)S(1)}, bf16[2,6,16,768]{3,0,2,1:T(2,128)(2,1)S(1)}, u32[]{:S(2)}, u32[]{:S(2)}) %collective-permute-start.8) | collective-permute-done | bytes 294944 | tf_op jit(solution)/shard_map/ppermute | solution.py:170
  147.1 2.1 %fusion.3 = bf16[2,16,16,768]{3,0,2,1:T(2,128)(2,1)S(1)} fusion(f32[2,28,16,768]{3,0,2,1:T(2,128)} %get-tuple-element.17, bf16[2,6,16,768]{3,0,2,1:T(2,128)(2,1)S(1)} %collective-permute-done.9, bf16[2,6,16,768]{3,0,2,1:T(2,128)(2,1)} %copy-done.19), kind=kLoop, calls=%fused_computation.8 | loop fusion | flops 1966080 | bytes 2949120 | tf_op jit(solution)/shard_map/convert_element_type | solution.py:255
  153.7 2.8 %maximum_convert_fusion = f32[768,1536]{1,0:T(8,128)} fusion(bf16[384,1536]{1,0:T(8,128)(2,1)S(1)} %get-tuple-element.19, bf16[384,1536]{1,0:T(8,128)(2,1)S(1)} %get-tuple-element.18), kind=kLoop, calls=%fused_computation.5 | loop fusion | flops 4718592 | bytes 7077888 | tf_op jit(solution)/shard_map/convert_element_type | solution.py:226
  (101 shorter events, 42.4 us)
Async XLA Ops:
  0.6 88.2 %copy-start = (bf16[768,1536]{1,0:T(8,128)(2,1)S(1)}, bf16[768,1536]{1,0:T(8,128)(2,1)}, u32[]{:S(2)}) copy-start(bf16[768,1536]{1,0:T(8,128)(2,1)} %param.12) | copy-start | bytes 7077892
  0.6 11.1 %copy-start.4 = (bf16[16,16,768]{2,1,0:T(8,128)(2,1)S(1)}, bf16[16,16,768]{2,1,0:T(8,128)(2,1)}, u32[]{:S(2)}) copy-start(bf16[16,16,768]{2,1,0:T(8,128)(2,1)} %param.10) | copy-start | bytes 1179652
  1.8 10.7 %copy-start.3 = (bf16[16,16,768]{2,1,0:T(8,128)(2,1)S(1)}, bf16[16,16,768]{2,1,0:T(8,128)(2,1)}, u32[]{:S(2)}) copy-start(bf16[16,16,768]{2,1,0:T(8,128)(2,1)} %param.9) | copy-start | bytes 1179652
  3.6 24.6 %collective-permute-start = (bf16[2,96,768]{2,1,0:T(8,128)(2,1)}, bf16[2,96,768]{2,1,0:T(8,128)(2,1)S(1)}, u32[]{:S(2)}, u32[]{:S(2)}) collective-permute-start(bf16[2,96,768]{2,1,0:T(8,128)(2,1)} %pad_maximum_fusion), channel_id=1, source_target_pairs={{0,32},{32,64},{64,96},{96,128},{128,160},{160,192},{192,224},{1,3... | collective-permute-start | bytes 884744 | tf_op jit(solution)/shard_map/ppermute | solution.py:170
  7.6 19.2 %collective-permute-start.1 = (bf16[2,96,768]{2,1,0:T(8,128)(2,1)}, bf16[2,96,768]{2,1,0:T(8,128)(2,1)}, u32[]{:S(2)}, u32[]{:S(2)}) collective-permute-start(bf16[2,96,768]{2,1,0:T(8,128)(2,1)} %pad_maximum_fusion.1), channel_id=1, source_target_pairs={{32,0},{64,32},{96,64},{128,96},{160,128},{192,160},{224,192},{33,... | collective-permute-start | bytes 884744 | tf_op jit(solution)/shard_map/ppermute | solution.py:170
  13.3 13.3 %copy-start.22 = (s32[2,128]{1,0:T(2,128)S(1)}, s32[2,128]{1,0:T(2,128)}, u32[]{:S(2)}) copy-start(s32[2,128]{1,0:T(2,128)} %constant.47.clone) | copy-start | bytes 3076
  13.3 13.4 %copy-start.21 = (s32[2,576]{1,0:T(2,128)S(1)}, s32[2,576]{1,0:T(2,128)}, u32[]{:S(2)}) copy-start(s32[2,576]{1,0:T(2,128)} %constant.48.clone) | copy-start | bytes 13828
  18.4 22.6 %collective-permute-start.5 = (bf16[2,96,768]{2,1,0:T(8,128)(2,1)}, bf16[2,96,768]{2,1,0:T(8,128)(2,1)}, u32[]{:S(2)}, u32[]{:S(2)}) collective-permute-start(bf16[2,96,768]{2,1,0:T(8,128)(2,1)} %pad_maximum_fusion.3), channel_id=1, source_target_pairs={{0,31},{1,0},{2,1},{3,2},{4,3},{5,4},{6,5},{7,6},{8,7},{9,8},{10,9... | collective-permute-start | bytes 884744 | tf_op jit(solution)/shard_map/ppermute | solution.py:175
  24.6 16.3 %collective-permute-start.3 = (bf16[2,96,768]{2,1,0:T(8,128)(2,1)}, bf16[2,96,768]{2,1,0:T(8,128)(2,1)}, u32[]{:S(2)}, u32[]{:S(2)}) collective-permute-start(bf16[2,96,768]{2,1,0:T(8,128)(2,1)} %pad_maximum_fusion.2), channel_id=1, source_target_pairs={{0,1},{1,2},{2,3},{3,4},{4,5},{5,6},{6,7},{7,8},{8,9},{9,10},{10,1... | collective-permute-start | bytes 884744 | tf_op jit(solution)/shard_map/ppermute | solution.py:175
  29.8 7.2 %collective-permute-start.4 = (bf16[2,2,36,768]{3,2,0,1:T(8,128)(2,1)S(1)}, bf16[2,2,36,768]{3,2,0,1:T(8,128)(2,1)S(1)}, u32[]{:S(2)}, u32[]{:S(2)}) collective-permute-start(bf16[2,2,36,768]{3,2,0,1:T(8,128)(2,1)S(1)} %copy.22), channel_id=1, source_target_pairs={{0,31},{1,0},{2,1},{3,2},{4,3},{5,4},{6,5},{7,6},{8,7},{9,8},{10,9... | collective-permute-start | bytes 663560 | tf_op jit(solution)/shard_map/ppermute | solution.py:175
  34.4 8.0 %copy-start.5 = (f32[2,576,128]{2,1,0:T(8,128)}, f32[2,576,128]{2,1,0:T(8,128)S(1)}, u32[]{:S(2)}) copy-start(f32[2,576,128]{2,1,0:T(8,128)S(1)} %and_select_fusion.bias_ref) | copy-start | bytes 1769476
  34.5 6.4 %collective-permute-start.2 = (bf16[2,2,36,768]{3,2,0,1:T(8,128)(2,1)S(1)}, bf16[2,2,36,768]{3,2,0,1:T(8,128)(2,1)S(1)}, u32[]{:S(2)}, u32[]{:S(2)}) collective-permute-start(bf16[2,2,36,768]{3,2,0,1:T(8,128)(2,1)S(1)} %copy.21), channel_id=1, source_target_pairs={{0,1},{1,2},{2,3},{3,4},{4,5},{5,6},{6,7},{7,8},{8,9},{9,10},{10,1... | collective-permute-start | bytes 663560 | tf_op jit(solution)/shard_map/ppermute | solution.py:175
  42.4 6.6 %copy-start.18 = (bf16[16,16,1536]{2,1,0:T(8,128)(2,1)S(1)}, bf16[16,16,1536]{2,1,0:T(8,128)(2,1)}, u32[]{:S(2)}) copy-start(bf16[16,16,1536]{2,1,0:T(8,128)(2,1)} %param.11) | copy-start | bytes 2359300
  50.5 11.1 %collective-permute-start.10 = (bf16[384,1536]{1,0:T(8,128)(2,1)}, bf16[384,1536]{1,0:T(8,128)(2,1)}, u32[]{:S(2)}, u32[]{:S(2)}) collective-permute-start(bf16[384,1536]{1,0:T(8,128)(2,1)} %convolution_convert_fusion), channel_id=1, source_target_pairs={{0,1},{1,0},{2,3},{3,2},{4,5},{5,4},{6,7},{7,6},{8,9},{9,8},{10,11... | collective-permute-start | bytes 3538952 | tf_op jit(solution)/shard_map/ppermute | solution.py:179
  85.3 3.3 %collective-permute-start.11 = (bf16[24,1536]{1,0:T(8,128)(2,1)S(1)}, bf16[24,1536]{1,0:T(8,128)(2,1)S(1)}, u32[]{:S(2)}, u32[]{:S(2)}) collective-permute-start(bf16[24,1536]{1,0:T(8,128)(2,1)S(1)} %reduce_sum.12), channel_id=1, source_target_pairs={{0,4},{4,0},{8,12},{12,8},{16,20},{20,16},{24,28},{28,24},{1,5},{5... | collective-permute-start | bytes 221192 | tf_op jit(solution)/shard_map/ppermute | solution.py:179
  88.6 6.4 %copy-start.6 = (f32[2,576,128]{2,1,0:T(8,128)S(1)}, f32[2,576,128]{2,1,0:T(8,128)}, u32[]{:S(2)}) copy-start(f32[2,576,128]{2,1,0:T(8,128)} %copy-done.5) | copy-start | bytes 1769476
  88.7 4.7 %collective-permute-start.12 = (bf16[24,1536]{1,0:T(8,128)(2,1)S(1)}, bf16[24,1536]{1,0:T(8,128)(2,1)S(1)}, u32[]{:S(2)}, u32[]{:S(2)}) collective-permute-start(bf16[24,1536]{1,0:T(8,128)(2,1)S(1)} %add_convert_fusion.2), channel_id=1, source_target_pairs={{0,8},{4,12},{8,0},{12,4},{16,24},{20,28},{24,16},{28,20},{1,9},{5... | collective-permute-start | bytes 221192 | tf_op jit(solution)/shard_map/ppermute | solution.py:179
  93.4 17.7 %collective-permute-start.13 = (bf16[24,1536]{1,0:T(8,128)(2,1)S(1)}, bf16[24,1536]{1,0:T(8,128)(2,1)S(1)}, u32[]{:S(2)}, u32[]{:S(2)}) collective-permute-start(bf16[24,1536]{1,0:T(8,128)(2,1)S(1)} %add_convert_fusion.1), channel_id=1, source_target_pairs={{0,16},{4,20},{8,24},{12,28},{16,0},{20,4},{24,8},{28,12},{1,17},{... | collective-permute-start | bytes 221192 | tf_op jit(solution)/shard_map/ppermute | solution.py:179
  105.4 21.2 %collective-permute-start.7 = (bf16[2,176,768]{2,1,0:T(8,128)(2,1)}, bf16[2,176,768]{2,1,0:T(8,128)(2,1)S(1)}, u32[]{:S(2)}, u32[]{:S(2)}) collective-permute-start(bf16[2,176,768]{2,1,0:T(8,128)(2,1)} %get-tuple-element.14), channel_id=1, source_target_pairs={{0,31},{1,0},{2,1},{3,2},{4,3},{5,4},{6,5},{7,6},{8,7},{9,8},{10,9... | collective-permute-start | bytes 1622024 | tf_op jit(solution)/shard_map/ppermute | solution.py:175
  109.9 17.2 %collective-permute-start.6 = (bf16[2,176,768]{2,1,0:T(8,128)(2,1)}, bf16[2,176,768]{2,1,0:T(8,128)(2,1)}, u32[]{:S(2)}, u32[]{:S(2)}) collective-permute-start(bf16[2,176,768]{2,1,0:T(8,128)(2,1)} %get-tuple-element.13), channel_id=1, source_target_pairs={{0,1},{1,2},{2,3},{3,4},{4,5},{5,6},{6,7},{7,8},{8,9},{9,10},{10,1... | collective-permute-start | bytes 1622024 | tf_op jit(solution)/shard_map/ppermute | solution.py:175
  112.2 26.8 %all-to-all-start.1 = ((bf16[16,24,1536]{2,1,0:T(8,128)(2,1)}), bf16[16,24,1536]{2,1,0:T(8,128)(2,1)}, u32[]{:S(2)}, u32[]{:S(2)}) async-start(bf16[16,24,1536]{2,1,0:T(8,128)(2,1)} %broadcast_in_dim.22), calls=%async_computation.1 | async-start | bytes 2359296 | tf_op jit(solution)/shard_map/all_to_all | solution.py:219
  133.8 8.6 %collective-permute-start.9 = (bf16[2,6,16,768]{3,0,2,1:T(2,128)(2,1)}, bf16[2,6,16,768]{3,0,2,1:T(2,128)(2,1)S(1)}, u32[]{:S(2)}, u32[]{:S(2)}) collective-permute-start(bf16[2,6,16,768]{3,0,2,1:T(2,128)(2,1)} %get-tuple-element.21), channel_id=1, source_target_pairs={{32,0},{64,32},{96,64},{128,96},{160,128},{192,160},{224,192},{33,... | collective-permute-start | bytes 884744 | tf_op jit(solution)/shard_map/ppermute | solution.py:170
  136.3 10.1 %collective-permute-start.8 = (bf16[2,6,16,768]{3,0,2,1:T(2,128)(2,1)S(1)}, bf16[2,6,16,768]{3,0,2,1:T(2,128)(2,1)S(1)}, u32[]{:S(2)}, u32[]{:S(2)}) collective-permute-start(bf16[2,6,16,768]{3,0,2,1:T(2,128)(2,1)S(1)} %get-tuple-element.20), channel_id=1, source_target_pairs={{0,32},{32,64},{64,96},{96,128},{128,160},{160,192},{192,224},{1,3... | collective-permute-start | bytes 884744 | tf_op jit(solution)/shard_map/ppermute | solution.py:170
  139.1 12.9 %collective-permute-start.14 = (bf16[384,1536]{1,0:T(8,128)(2,1)}, bf16[384,1536]{1,0:T(8,128)(2,1)}, u32[]{:S(2)}, u32[]{:S(2)}) collective-permute-start(bf16[384,1536]{1,0:T(8,128)(2,1)} %bitcast.21), channel_id=1, source_target_pairs={{0,1},{1,0},{2,3},{3,2},{4,5},{5,4},{6,7},{7,6},{8,9},{9,8},{10,11... | collective-permute-start | bytes 3538952 | tf_op jit(solution)/shard_map/ppermute | solution.py:179
  (15 other events, 66.9 us)

commit v2 on v1

v2 whole, which is shorter than its diff:
```python
import jax
import jax.numpy as jnp
import numpy as np
from jax import lax
from jax.experimental import pallas as pl
from jax.experimental.pallas import tpu as pltpu
from jax.sharding import Mesh, PartitionSpec as P

HEADS = 6
HALF_HEADS = HEADS // 2
HEAD_DIM = 128
WIDTH = 1536
WIN = 13
REACH = 6
ROWS = 16
COLS = 16
CHANNELS = HEADS * HEAD_DIM
HALF = CHANNELS // 2
TOKENS = ROWS * COLS
EDGE = REACH * COLS
SPAN = ROWS + 2 * REACH
MID = SPAN * COLS
CORNER = 80
CORNER_TILE = 48
SIDE = EDGE + CORNER
TILES = 2
TILE_Q = TOKENS // TILES
MID_TILE = 320
SIDE_TILE = EDGE + CORNER_TILE
KEYS = MID_TILE + 2 * SIDE_TILE
MID_STARTS = (0, 128)
CORNER_STARTS = (0, CORNER - CORNER_TILE)
SCALE = HEAD_DIM ** -0.5
LAT = ("xl", "y")
LON = ("z", "xh", "core")
HALOS = 6
PLANE = ("xl", "y", "xh")
F32 = jnp.float32
BF16 = jnp.bfloat16
FULL = pltpu.CompilerParams(vmem_limit_bytes=60 * 1024 * 1024)
SMALL = pltpu.CompilerParams(vmem_limit_bytes=16 * 1024 * 1024)


def side_places():
    count = REACH * REACH
    own_rows, own_cols = np.divmod(np.arange(EDGE), REACH)
    rows, cols = np.divmod(np.arange(count), REACH)
    spare = np.zeros(CORNER - 2 * count, np.int64)
    return (
        np.concatenate([REACH + own_rows, rows, REACH + ROWS + rows, spare]),
        np.concatenate([own_cols, cols, cols, spare]),
        np.arange(SIDE) < EDGE + 2 * count,
    )


def key_places(core):
    mid_rows, mid_cols = np.divmod(np.arange(MID), COLS)
    side_rows, side_cols, used = side_places()
    west_cols = np.where(used, side_cols - REACH, 1000)
    east_cols = np.where(used, side_cols + COLS, 1000)
    chip_cols, next_cols = (east_cols, west_cols) if core == 0 else (west_cols, east_cols)
    rows, cols = [], []
    for mid, corner in zip(MID_STARTS, CORNER_STARTS):
        mids = np.arange(mid, mid + MID_TILE)
        sides = np.concatenate([np.arange(EDGE), EDGE + corner + np.arange(CORNER_TILE)])
        rows.append(np.concatenate([mid_rows[mids], side_rows[sides], side_rows[sides]]) - REACH)
        cols.append(np.concatenate([mid_cols[mids], chip_cols[sides], next_cols[sides]]))
    return np.stack(rows), np.stack(cols)


def window_bias(core, first_row, total_rows):
    (rows, cols), (_, other_cols) = key_places(0), key_places(1)
    cols = jnp.where(core == 0, cols, other_cols)
    query_rows, query_cols = np.divmod(np.arange(TOKENS).reshape(TILES, TILE_Q), COLS)
    start = jnp.clip(first_row + query_rows - REACH, 0, total_rows - WIN)[:, None, :]
    key_rows = (first_row + rows)[:, :, None]
    near = jnp.abs(cols[:, :, None] - query_cols[:, None, :]) <= REACH
    keep = (key_rows >= start) & (key_rows < start + WIN) & near
    return jnp.where(keep, 0.0, -1e30).astype(F32)


def sent_cols(core):
    return (COLS - REACH, 0) if core == 0 else (0, COLS - REACH)


def strip_picks():
    picks = np.zeros((2, 2 * EDGE, TOKENS), np.float32)
    rows, cols = np.divmod(np.arange(EDGE), REACH)
    for core in range(2):
        for slot, col in enumerate(sent_cols(core)):
            picks[core, slot * EDGE + np.arange(EDGE), rows * COLS + cols + col] = 1
    return picks


def corner_picks():
    count = REACH * REACH
    picks = np.zeros((2, 2 * CORNER, 2 * EDGE), np.float32)
    rows, cols = np.divmod(np.arange(count), REACH)
    for core in range(2):
        for slot, col in enumerate(sent_cols(core)):
            for pole in range(2):
                at = slot * CORNER + pole * count + np.arange(count)
                picks[core, at, pole * EDGE + rows * COLS + cols + col] = 1
    return picks


def dot(a, b, dims):
    return lax.dot_general(a, b, (dims, ((), ())), preferred_element_type=F32)


def with_picks(kernel, core, picks, arrays, in_specs, out_specs, out_shape, steps, bytes_accessed):
    picks = jnp.asarray(picks, BF16)
    own = pl.BlockSpec((None,) + picks.shape[1:], lambda h, at: (at[0], 0, 0))
    return pl.pallas_call(
        kernel,
        grid_spec=pltpu.PrefetchScalarGridSpec(
            num_scalar_prefetch=1, grid=(steps,), in_specs=[own] + in_specs, out_specs=out_specs
        ),
        out_shape=out_shape,
        compiler_params=FULL,
        cost_estimate=pl.CostEstimate(flops=10**9, bytes_accessed=bytes_accessed, transcendentals=0),
    )(core, picks, *arrays)


def strip_kernel(core_ref, picks_ref, k_ref, v_ref, north_ref, south_ref, chip_ref, next_ref):
    for slot, ref in enumerate((k_ref, v_ref)):
        north_ref[slot] = ref[TOKENS - EDGE :, :]
        south_ref[slot] = ref[:EDGE, :]
        picked = dot(picks_ref[...], ref[...], ((1,), (0,))).astype(BF16)
        chip_ref[slot] = picked[:EDGE]
        next_ref[slot] = picked[EDGE:]


def strips_of(core, k, v):
    return with_picks(
        strip_kernel, core, strip_picks(), (k, v),
        [by_heads((), TOKENS, HEADS)] * 2, [by_heads((2,), EDGE, HEADS)] * 4,
        [jax.ShapeDtypeStruct((2, EDGE, CHANNELS), BF16)] * 4, 1, 2 * 10**6,
    )


def corner_kernel(core_ref, picks_ref, north_ref, south_ref, chip_ref, next_ref):
    for slot in range(2):
        poles = jnp.concatenate([north_ref[slot], south_ref[slot]], axis=0)
        picked = dot(picks_ref[...], poles, ((1,), (0,))).astype(BF16)
        chip_ref[slot] = picked[:CORNER]
        next_ref[slot] = picked[CORNER:]


def corners_of(core, north, south):
    return with_picks(
        corner_kernel, core, corner_picks(), (north, south),
        [by_heads((2,), EDGE, HEADS)] * 2, [by_heads((2,), CORNER, HEADS)] * 2,
        [jax.ShapeDtypeStruct((2, CORNER, CHANNELS), BF16)] * 2, 1, 10**6,
    )


def tile_keys(tile, own, north, south, chip, beyond, chip_corner, beyond_corner):
    corner = slice(CORNER_STARTS[tile], CORNER_STARTS[tile] + CORNER_TILE)
    if tile == 0:
        mid = [north, own[: MID_TILE - EDGE]]
    else:
        mid = [own[TOKENS - (MID_TILE - EDGE) :], south]
    return jnp.concatenate(mid + [chip, chip_corner[corner], beyond, beyond_corner[corner]], axis=0)


def forward_kernel(q_ref, k_ref, v_ref, *refs):
    halo_refs, (bias_ref, out_ref, lse_ref) = refs[:HALOS], refs[HALOS:]
    keys = (k_ref[...], *(ref[0] for ref in halo_refs))
    values = (v_ref[...], *(ref[1] for ref in halo_refs))
    for tile in range(TILES):
        span = slice(tile * TILE_Q, (tile + 1) * TILE_Q)
        scores = dot(tile_keys(tile, *keys), q_ref[span, :], ((1,), (1,))) * SCALE + bias_ref[tile]
        top = jnp.max(scores, axis=0, keepdims=True)
        exponent = jnp.exp(scores - top)
        total = jnp.sum(exponent, axis=0, keepdims=True)
        prob = (exponent * (1.0 / total)).astype(BF16)
        out_ref[span, :] = dot(prob, tile_keys(tile, *values), ((0,), (0,))).astype(BF16)
        lse_ref[0, tile : tile + 1, :] = top + jnp.log(total)


def backward_kernel(q_ref, k_ref, v_ref, *refs):
    halo_refs, (bias_ref, g_ref, lse_ref) = refs[:HALOS], refs[HALOS : HALOS + 3]
    dq_ref, own_ref, poles_ref, dchip_ref, dnext_ref, prob_s, score_s = refs[HALOS + 3 :]

    @pl.when(pl.program_id(0) == 0)
    def _():
        prob_s[...] = jnp.zeros_like(prob_s)
        score_s[...] = jnp.zeros_like(score_s)

    keys = (k_ref[...], *(ref[0] for ref in halo_refs))
    values = (v_ref[...], *(ref[1] for ref in halo_refs))
    for tile in range(TILES):
        span = slice(tile * TILE_Q, (tile + 1) * TILE_Q)
        key_tile = tile_keys(tile, *keys)
        scores = dot(key_tile, q_ref[span, :], ((1,), (1,))) * SCALE + bias_ref[tile]
        prob = jnp.exp(scores - lse_ref[0, tile : tile + 1, :])
        grad_prob = dot(tile_keys(tile, *values), g_ref[span, :], ((1,), (1,)))
        delta = jnp.sum(prob * grad_prob, axis=0, keepdims=True)
        grad_score = (prob * (grad_prob - delta) * SCALE).astype(BF16)
        dq_ref[span, :] = dot(grad_score, key_tile, ((0,), (0,))).astype(BF16)
        mid, corner = MID_STARTS[tile], CORNER_STARTS[tile]
        for part, scratch in ((prob.astype(BF16), prob_s), (grad_score, score_s)):
            scratch[mid : mid + MID_TILE, span] = part[:MID_TILE]
            for at, low in ((MID, MID_TILE), (MID + SIDE, MID_TILE + SIDE_TILE)):
                scratch[at : at + EDGE, span] = part[low : low + EDGE]
                at = at + EDGE + corner
                scratch[at : at + CORNER_TILE, span] = part[low + EDGE : low + SIDE_TILE]
    for slot, scratch, other in ((0, score_s, q_ref), (1, prob_s, g_ref)):
        grads = dot(scratch[...], other[...], ((1,), (0,)))
        poles_ref[slot, :EDGE] = grads[:EDGE]
        own_ref[slot] = grads[EDGE : EDGE + TOKENS]
        poles_ref[slot, EDGE:] = grads[EDGE + TOKENS : MID]
        dchip_ref[slot] = grads[MID : MID + SIDE].astype(BF16)
        dnext_ref[slot] = grads[MID + SIDE :].astype(BF16)


def by_heads(lead, rows, heads=1):
    shape = lead + (rows, heads * HEAD_DIM)
    return pl.BlockSpec(shape, lambda h, *at: (0,) * (len(lead) + 1) + (h,))


def input_specs():
    tokens = by_heads((), TOKENS)
    halos = [by_heads((2,), EDGE)] * 4 + [by_heads((2,), CORNER)] * 2
    bias = pl.BlockSpec((TILES, KEYS, TILE_Q), lambda h: (0, 0, 0))
    return [tokens] * 3 + halos + [bias]


def lse_spec():
    return pl.BlockSpec((1, 8, TILE_Q), lambda h: (h, 0, 0))


def forward_attention(q, k, v, halos, bias):
    return pl.pallas_call(
        forward_kernel,
        grid=(HEADS,),
        in_specs=input_specs(),
        out_specs=[by_heads((), TOKENS), lse_spec()],
        out_shape=[
            jax.ShapeDtypeStruct((TOKENS, CHANNELS), BF16),
            jax.ShapeDtypeStruct((HEADS, 8, TILE_Q), F32),
        ],
        compiler_params=FULL,
        cost_estimate=pl.CostEstimate(flops=2 * 10**9, bytes_accessed=6 * 10**6, transcendentals=10**6),
    )(q, k, v, *halos, bias)


def backward_attention(q, k, v, halos, bias, g, lse):
    keys = MID + 2 * SIDE
    return pl.pallas_call(
        backward_kernel,
        grid=(HEADS,),
        in_specs=input_specs() + [by_heads((), TOKENS), lse_spec()],
        out_specs=[by_heads((), TOKENS)] + [by_heads((2,), rows) for rows in (TOKENS, 2 * EDGE, SIDE, SIDE)],
        out_shape=[
            jax.ShapeDtypeStruct((TOKENS, CHANNELS), BF16),
            jax.ShapeDtypeStruct((2, TOKENS, CHANNELS), F32),
            jax.ShapeDtypeStruct((2, 2 * EDGE, CHANNELS), F32),
            jax.ShapeDtypeStruct((2, SIDE, CHANNELS), BF16),
            jax.ShapeDtypeStruct((2, SIDE, CHANNELS), BF16),
        ],
        scratch_shapes=[pltpu.VMEM((keys, TOKENS), BF16), pltpu.VMEM((keys, TOKENS), BF16)],
        compiler_params=FULL,
        cost_estimate=pl.CostEstimate(flops=6 * 10**9, bytes_accessed=12 * 10**6, transcendentals=10**6),
    )(q, k, v, *halos, bias, g, lse)


def merge_poles_kernel(core_ref, spread_ref, poles_ref, chip_ref, next_ref, north_ref, south_ref):
    for slot in range(2):
        corners = jnp.concatenate([chip_ref[slot, EDGE:], next_ref[slot, EDGE:]], axis=0)
        poles = (poles_ref[slot] + dot(spread_ref[...], corners, ((1,), (0,)))).astype(BF16)
        north_ref[slot] = poles[:EDGE]
        south_ref[slot] = poles[EDGE:]


def merge_poles(core, poles, from_chip, from_next):
    heads = 3
    return with_picks(
        merge_poles_kernel, core, corner_picks().transpose(0, 2, 1), (poles, from_chip, from_next),
        [by_heads((2,), rows, heads) for rows in (2 * EDGE, SIDE, SIDE)], [by_heads((2,), EDGE, heads)] * 2,
        [jax.ShapeDtypeStruct((2, EDGE, CHANNELS), BF16)] * 2, HEADS // heads, 4 * 10**6,
    )


def merge_own_kernel(
    core_ref, spread_ref, own_ref, chip_ref, next_ref, from_north_ref, from_south_ref, dk_ref, dv_ref
):
    low, high = EDGE, TOKENS - EDGE
    for slot, out_ref in enumerate((dk_ref, dv_ref)):
        sides = jnp.concatenate([chip_ref[slot, :EDGE], next_ref[slot, :EDGE]], axis=0)
        own = own_ref[slot] + dot(spread_ref[...], sides, ((1,), (0,)))
        out_ref[:low, :] = (own[:low] + from_north_ref[slot].astype(F32)).astype(BF16)
        out_ref[low:high, :] = own[low:high].astype(BF16)
        out_ref[high:, :] = (own[high:] + from_south_ref[slot].astype(F32)).astype(BF16)


def merge_own(core, own, from_chip, from_next, from_north, from_south):
    heads = 3
    return with_picks(
        merge_own_kernel, core, strip_picks().transpose(0, 2, 1), (own, from_chip, from_next, from_north, from_south),
        [by_heads((2,), rows, heads) for rows in (TOKENS, SIDE, SIDE, EDGE, EDGE)], [by_heads((), TOKENS, heads)] * 2,
        [jax.ShapeDtypeStruct((TOKENS, CHANNELS), BF16)] * 2, HEADS // heads, 6 * 10**6,
    )


def widen_kernel(which_ref, half_ref, *refs):
    refs[-1][...] = half_ref[...].astype(F32)


def widen_half(half, which, earlier=None):
    block = (HEAD_DIM, WIDTH)
    rest = [] if earlier is None else [earlier]
    return pl.pallas_call(
        widen_kernel,
        grid_spec=pltpu.PrefetchScalarGridSpec(
            num_scalar_prefetch=1,
            grid=(HALF_HEADS,),
            in_specs=[pl.BlockSpec(block, lambda h, at: (h, 0))] + [pl.BlockSpec(memory_space=pl.ANY)] * len(rest),
            out_specs=pl.BlockSpec(block, lambda h, at: (at[0] * HALF_HEADS + h, 0)),
        ),
        out_shape=jax.ShapeDtypeStruct((CHANNELS, WIDTH), F32),
        input_output_aliases={2: 0} if rest else {},
        compiler_params=SMALL,
        cost_estimate=pl.CostEstimate(flops=10**6, bytes_accessed=4 * 10**6, transcendentals=0),
    )(which, half, *rest)


def along_lat(block, by):
    bands = lax.axis_size(LAT)
    return lax.ppermute(block, LAT, [(i, i + by) for i in range(bands) if 0 <= i + by < bands])


def with_next_chip(block):
    strips = lax.axis_size(LON)
    return lax.ppermute(block, LON, [(j, (j + 2 * (j % 2) - 1) % strips) for j in range(strips)])


def swapped(block, axis, bit):
    return lax.ppermute(block, axis, [(i, i ^ bit) for i in range(lax.axis_size(axis))])


def with_chip(block):
    return swapped(block, "core", 1)


def halos_of(core, k, v):
    north, south, chip, beyond = strips_of(core, k, v)
    north, south = along_lat(north, 1), along_lat(south, -1)
    chip, beyond = with_chip(chip), with_next_chip(beyond)
    chip_corner, beyond_corner = corners_of(core, north, south)
    return north, south, chip, beyond, with_chip(chip_corner), with_next_chip(beyond_corner)


def plane_sum(pair):
    group = lax.axis_size(PLANE)
    return lax.all_to_all(
        pair.reshape(group, HALF // group, WIDTH), PLANE, split_axis=0, concat_axis=0, tiled=True
    )


def local(queries, key_vectors, value_vectors, grad_output, out_weight):
    core = lax.axis_index("core").astype(jnp.int32)
    q = queries.reshape(TOKENS, CHANNELS)
    k = key_vectors.reshape(TOKENS, CHANNELS)
    v = value_vectors.reshape(TOKENS, CHANNELS)
    grad_rows = grad_output.reshape(TOKENS, WIDTH)
    which = core.reshape(1)
    halos = halos_of(which, k, v)
    bias = window_bias(core, lax.axis_index(LAT) * ROWS, ROWS * lax.axis_size(LAT))
    grad_attn = dot(grad_rows, out_weight, ((1,), (1,))).astype(BF16)

    attended, lse = forward_attention(q, k, v, halos, bias)

    def term(half):
        return dot(lax.dynamic_slice_in_dim(attended, half * HALF, HALF, axis=1), grad_rows, ((0,), (0,)))

    received = swapped(term(1 - core).astype(BF16), "core", 1)
    pieces = plane_sum((term(core) + received.astype(F32)).astype(BF16))
    grad_q, own, poles, side_chip, side_next = backward_attention(q, k, v, halos, bias, grad_attn, lse)
    from_chip, from_next = with_chip(side_chip), with_next_chip(side_next)

    def z_step(total, bit):
        part = total.astype(BF16)
        return part.astype(F32) + swapped(part, "z", bit).astype(F32)

    pieces, grad_q = lax.optimization_barrier((pieces, grad_q))
    total = jnp.sum(pieces.astype(F32), axis=0)
    total = z_step(total, 1)
    total, from_chip, from_next = lax.optimization_barrier((total, from_chip, from_next))
    north, south = merge_poles(which, poles, from_chip, from_next)
    total = z_step(z_step(total, 2), 4)
    total, north, south = lax.optimization_barrier((total, north, south))
    group = lax.axis_size(PLANE)
    part = jnp.broadcast_to(total.astype(BF16)[None], (group, HALF // group, WIDTH))
    whole = plane_sum(part).reshape(HALF, WIDTH)
    from_north, from_south = along_lat(south, 1), along_lat(north, -1)
    whole, from_north, from_south = lax.optimization_barrier((whole, from_north, from_south))
    grad_k, grad_v = merge_own(which, own, from_chip, from_next, from_north, from_south)
    other = swapped(whole, "core", 1)
    grad_weight = widen_half(whole, which)
    grad_weight = widen_half(other, 1 - which, grad_weight)
    shape = queries.shape
    return grad_q.reshape(shape), grad_k.reshape(shape), grad_v.reshape(shape), grad_weight


def solution(mesh):
    fine = Mesh(mesh.devices.reshape(2, 4, 8, 2, 2), LAT + LON)
    spread = P(LAT, LON, None)
    return jax.shard_map(
        local,
        mesh=fine,
        in_specs=(spread, spread, spread, spread, P()),
        out_specs=(spread, spread, spread, P()),
        check_vma=False,
    )
```

time: 158 us -> 142 us (0.90)
  blocking collectives: 20.3 us -> 0 us
  local copies, waits for them, and re-layouts: 22.7 us -> 3.27 us
  Pallas kernels: 14.8 us -> 31.6 us
  other arithmetic: 19.4 us -> 2.96 us
  starting transfers between devices: 42.6 us -> 54.6 us
  waiting for transfers between devices: 30.1 us -> 39.6 us
  matrix products: 5.59 us -> 7.97 us
    all_to_all x1 -> x0, blocking collectives: 20.3 us -> none  [sum_of_weight_terms(): lax.all_to_all(pair.reshape(group, half // group, WIDTH), PLANE, split_ax...]
    pallas_call x2 -> x8, Pallas kernels: 14.8 us -> 31.6 us  [the longest x4 10.1 us: with_picks(): pl.pallas_call(kernel, grid_spec=pltpu.PrefetchScalarGridSpec(num_scalar_...]
    ppermute x5 -> x8, starting transfers between devices: 11.7 us -> 24.8 us  [swapped(): lax.ppermute(block, axis, [(i, i ^ bit) for i in range(lax.axis_size(axis...]
    another operation x6 -> x0, other arithmetic: 9.55 us -> none  [the longest x4 4.93 us: strip(): jnp.stack([keys[rows, cols], values[rows, cols]]).reshape(2, -1, CHANNELS)]
    slice x10 -> x0, local copies, waits for them, and re-layouts: 8.78 us -> none  [the longest x2 1.95 us: strip(): values[rows, cols]]
    another operation x6 -> x0, local copies, waits for them, and re-layouts: 8.63 us -> none  [the longest x4 6.57 us: strip(): jnp.stack([keys[rows, cols], values[rows, cols]]).reshape(2, -1, CHANNELS)]
    ppermute x10 -> x7, starting transfers between devices: 26 us -> 18.4 us  [the longest x4 14.8 us: along_lat(): lax.ppermute(block, LAT, [(i, i + by) for i in range(bands) if 0 <= i + b...]
    ppermute x10 -> x7, waiting for transfers between devices: 21.5 us -> 28.3 us  [the longest x4 14.9 us: along_lat(): lax.ppermute(block, LAT, [(i, i + by) for i in range(bands) if 0 <= i + b...]
  transfers between devices with their start and end apart: 16 -> 17, of which waited for: 8 -> 11; matrix products, arithmetic and copies ran while one was open for 20% -> 4% of each run, Pallas kernels for 6% -> 13%
where the time goes in v2:
time: 142 us; the launch traced here: 141 us
  starting transfers between devices  54.6 us (38%)
  waiting for transfers between devices  39.6 us (28%)
  Pallas kernels  31.6 us (22%)
  matrix products  7.97 us (6%)
  local copies, waits for them, and re-layouts  3.27 us (2%)
  other arithmetic  2.96 us (2%)
    ppermute x8, starting transfers between devices, swapped(): lax.ppermute(block, axis, [(i, i ^ bit) for i in range(lax.axis_size(axis...  24.8 us
    ppermute x4, waiting for transfers between devices, along_lat(): lax.ppermute(block, LAT, [(i, i + by) for i in range(bands) if 0 <= i + b...  14.9 us
    ppermute x4, starting transfers between devices, along_lat(): lax.ppermute(block, LAT, [(i, i + by) for i in range(bands) if 0 <= i + b...  14.8 us
    ppermute x3, waiting for transfers between devices, with_next_chip(): lax.ppermute(block, LON, [(j, (j + 2 * (j % 2) - 1) % strips) for j in ra...  13.4 us
    all_to_all x2, starting transfers between devices, plane_sum(): lax.all_to_all(pair.reshape(group, HALF // group, WIDTH), PLANE, split_ax...  11.4 us
    pallas_call x4, Pallas kernels, with_picks(): pl.pallas_call(kernel, grid_spec=pltpu.PrefetchScalarGridSpec(num_scalar_...  10.1 us
    pallas_call x1, Pallas kernels, backward_attention(): pl.pallas_call(backward_kernel, grid=(HEADS,), in_specs=input_specs() + [...  9.2 us
    dot_general x3, matrix products, dot(): return lax.dot_general(a, b, (dims, ((), ())), preferred_element_type=F32)  7.97 us
  transfers between devices with their start and end apart: 17, of which 11 were waited for; matrix products, arithmetic and copies ran while one was open for 4% of the time, Pallas kernels for 13%

profile of v2, /device:TPU:3, one launch (start us, length us, event | category | flops | bytes accessed | tf_op | source)
XLA Modules:
  0.0 140.8 jit_solution(17508337470973634193)
XLA Ops:
  0.7 2.6 %shard_map.165 = (bf16[2,96,768]{2,1,0:T(8,128)(2,1)}, bf16[2,96,768]{2,1,0:T(8,128)(2,1)}, bf16[2,96,768]{2,1,0:T(8,128)(2,1)}, bf16[2,96,768]{2,1,0:T(8,128)(2,1)}) custom-call(s32[1]{0:T(128)} %bitcast.3.core_ref.which_ref, bf16[2,192,256]{2,1,0:T(8,128)(2,1)} %constant.61.clone.picks_ref, bf16[256,768]{1,0:T(8,128)(2,1)} %bitcast.22, ...), custom_call_target="tpu_custom_call" | custom-call | flops 1000000000 | bytes 2000000 | tf_op jit(solution)/shard_map/pallas_call | solution.py:114
  3.3 3.2 %collective-permute-start = (bf16[2,96,768]{2,1,0:T(8,128)(2,1)}, bf16[2,96,768]{2,1,0:T(8,128)(2,1)S(1)}, u32[]{:S(2)}, u32[]{:S(2)}) collective-permute-start(bf16[2,96,768]{2,1,0:T(8,128)(2,1)} %get-tuple-element.32), channel_id=1, source_target_pairs={{0,32},{32,64},{64,96},{96,128},{128,160},{160,192},{192,224},{1,3... | collective-permute-start | bytes 884744 | tf_op jit(solution)/shard_map/ppermute | solution.py:331
  6.5 4.2 %collective-permute-start.1 = (bf16[2,96,768]{2,1,0:T(8,128)(2,1)}, bf16[2,96,768]{2,1,0:T(8,128)(2,1)S(1)}, u32[]{:S(2)}, u32[]{:S(2)}) collective-permute-start(bf16[2,96,768]{2,1,0:T(8,128)(2,1)} %get-tuple-element.33), channel_id=1, source_target_pairs={{32,0},{64,32},{96,64},{128,96},{160,128},{192,160},{224,192},{33,... | collective-permute-start | bytes 884744 | tf_op jit(solution)/shard_map/ppermute | solution.py:331
  19.2 6.5 %collective-permute-start.4 = (bf16[2,80,768]{2,1,0:T(8,128)(2,1)}, bf16[2,80,768]{2,1,0:T(8,128)(2,1)S(1)}, u32[]{:S(2)}, u32[]{:S(2)}) collective-permute-start(bf16[2,80,768]{2,1,0:T(8,128)(2,1)} %get-tuple-element.36), channel_id=1, source_target_pairs={{0,1},{1,0},{2,3},{3,2},{4,5},{5,4},{6,7},{7,6},{8,9},{9,8},{10,11... | collective-permute-start | bytes 737288 | tf_op jit(solution)/shard_map/ppermute | solution.py:340
  27.0 8.6 %collective-permute-done.5.refs_5_ = bf16[2,80,768]{2,1,0:T(8,128)(2,1)S(1)} collective-permute-done((bf16[2,80,768]{2,1,0:T(8,128)(2,1)}, bf16[2,80,768]{2,1,0:T(8,128)(2,1)S(1)}, u32[]{:S(2)}, u32[]{:S(2)}) %collective-permute-start.5) | collective-permute-done | bytes 245792 | tf_op jit(solution)/shard_map/ppermute | solution.py:336
  36.3 7.1 %shard_map.167 = (bf16[256,768]{1,0:T(8,128)(2,1)}, f32[6,8,128]{2,1,0:T(8,128)}) custom-call(bf16[256,768]{1,0:T(8,128)(2,1)} %bitcast.20, bf16[256,768]{1,0:T(8,128)(2,1)} %bitcast.23, bf16[256,768]{1,0:T(8,128)(2,1)} %bitcast.26, bf16[2,96,768]{2,1,0:T(8,128)(2,1)} %copy-done.8, bf16[2,96,768]{2,1,0:T(8,128)(2,1)} %copy-done.9, ...), custom_call_target="tpu_custom_call" | custom-call | flops 2000000000 | bytes 6000000 | tf_op jit(solution)/shard_map/pallas_call | solution.py:235
  46.2 2.9 %collective-permute-done.6 = bf16[384,1536]{1,0:T(8,128)(2,1)} collective-permute-done((bf16[384,1536]{1,0:T(8,128)(2,1)}, bf16[384,1536]{1,0:T(8,128)(2,1)}, u32[]{:S(2)}, u32[]{:S(2)}) %collective-permute-start.6) | collective-permute-done | bytes 1179680 | tf_op jit(solution)/shard_map/ppermute | solution.py:340
  49.1 2.8 %fusion = bf16[384,1536]{1,0:T(8,128)(2,1)} fusion(bf16[256,1536]{1,0:T(8,128)(2,1)S(1)} %bitcast.19, bf16[384,1536]{1,0:T(8,128)(2,1)} %collective-permute-done.6, bf16[256,768]{1,0:T(8,128)(2,1)S(1)} %copy-done.2, s32[]{:T(128)S(6)} %select_n.21), kind=kOutput, calls=%fused_computation.1 | convolution fusion | flops 303759360 | bytes 3342340 | tf_op jit(solution)/shard_map/dot_general | solution.py:108
  51.9 6.2 %all-to-all-start = ((bf16[16,24,1536]{2,1,0:T(8,128)(2,1)}), bf16[16,24,1536]{2,1,0:T(8,128)(2,1)S(1)}, u32[]{:S(2)}, u32[]{:S(2)}) async-start(bf16[16,24,1536]{2,1,0:T(8,128)(2,1)} %bitcast.16), calls=%async_computation | async-start | bytes 2359296 | tf_op jit(solution)/shard_map/all_to_all | solution.py:357
  58.1 2.7 %convolution_convert_fusion.1.refs_7_ = bf16[256,768]{1,0:T(8,128)(2,1)} fusion(bf16[256,1536]{1,0:T(8,128)(2,1)} %bitcast.17, bf16[768,1536]{1,0:T(8,128)(2,1)S(1)} %copy-done), kind=kOutput, calls=%fused_computation.3 | convolution fusion | flops 604176384 | bytes 3538944 | tf_op jit(solution)/shard_map/dot_general | solution.py:108
  60.8 9.2 %shard_map.168 = (bf16[256,768]{1,0:T(8,128)(2,1)}, f32[2,256,768]{2,1,0:T(8,128)}, f32[2,192,768]{2,1,0:T(8,128)}, bf16[2,176,768]{2,1,0:T(8,128)(2,1)}, bf16[2,176,768]{2,1,0:T(8,128)(2,1)}) custom-call(bf16[256,768]{1,0:T(8,128)(2,1)} %bitcast.21, bf16[256,768]{1,0:T(8,128)(2,1)} %bitcast.24, bf16[256,768]{1,0:T(8,128)(2,1)} %bitcast.27, ...), custom_call_target="tpu_custom_call" | custom-call | flops 6000000000 | bytes 12000000 | tf_op jit(solution)/shard_map/pallas_call | solution.py:251
  72.8 3.4 %all-to-all-done = bf16[16,24,1536]{2,1,0:T(8,128)(2,1)S(1)} async-done(((bf16[16,24,1536]{2,1,0:T(8,128)(2,1)}), bf16[16,24,1536]{2,1,0:T(8,128)(2,1)S(1)}, u32[]{:S(2)}, u32[]{:S(2)}) %all-to-all-start) | async-done | bytes 1179680 | tf_op jit(solution)/shard_map/all_to_all | solution.py:357
  78.5 3.2 %collective-permute-done.7 = bf16[24,1536]{1,0:T(8,128)(2,1)S(1)} collective-permute-done((bf16[24,1536]{1,0:T(8,128)(2,1)}, bf16[24,1536]{1,0:T(8,128)(2,1)S(1)}, u32[]{:S(2)}, u32[]{:S(2)}) %collective-permute-start.7) | collective-permute-done | bytes 73760 | tf_op jit(solution)/shard_map/ppermute | solution.py:340
  82.6 4.8 %collective-permute-done.9.next_ref = bf16[2,176,768]{2,1,0:T(8,128)(2,1)} collective-permute-done((bf16[2,176,768]{2,1,0:T(8,128)(2,1)}, bf16[2,176,768]{2,1,0:T(8,128)(2,1)}, u32[]{:S(2)}, u32[]{:S(2)}) %collective-permute-start.9) | collective-permute-done | bytes 540704 | tf_op jit(solution)/shard_map/ppermute | solution.py:336
  87.4 2.9 %collective-permute-start.10 = (bf16[24,1536]{1,0:T(8,128)(2,1)S(1)}, bf16[24,1536]{1,0:T(8,128)(2,1)S(1)}, u32[]{:S(2)}, u32[]{:S(2)}) collective-permute-start(bf16[24,1536]{1,0:T(8,128)(2,1)S(1)} %convert_add_fusion.1), channel_id=1, source_target_pairs={{0,8},{4,12},{8,0},{12,4},{16,24},{20,28},{24,16},{28,20},{1,9},{5... | collective-permute-start | bytes 221192 | tf_op jit(solution)/shard_map/ppermute | solution.py:340
  92.1 7.2 %collective-permute-start.11 = (bf16[24,1536]{1,0:T(8,128)(2,1)S(1)}, bf16[24,1536]{1,0:T(8,128)(2,1)S(1)}, u32[]{:S(2)}, u32[]{:S(2)}) collective-permute-start(bf16[24,1536]{1,0:T(8,128)(2,1)S(1)} %add_convert_fusion), channel_id=1, source_target_pairs={{0,16},{4,20},{8,24},{12,28},{16,0},{20,4},{24,8},{28,12},{1,17},{... | collective-permute-start | bytes 221192 | tf_op jit(solution)/shard_map/ppermute | solution.py:340
  99.2 2.5 %shard_map.169 = (bf16[2,96,768]{2,1,0:T(8,128)(2,1)}, bf16[2,96,768]{2,1,0:T(8,128)(2,1)}) custom-call(s32[1]{0:T(128)} %bitcast.3.core_ref.which_ref, bf16[2,192,160]{2,1,0:T(8,128)(2,1)} %constant.68.clone.spread_ref, f32[2,192,768]{2,1,0:T(8,128)} %get-tuple-element.49.poles_ref, bf16[2,176,768]{2,1,0:T(8,128)(2,1)} %collective-permute-done.8.chip_ref, ...), custom_call_target="tpu_custom_call" | custom-call | flops 1000000000 | bytes 4000000 | tf_op jit(solution)/shard_map/pallas_call | solution.py:114
  102.9 5.2 %all-to-all-start.1 = ((bf16[16,24,1536]{2,1,0:T(8,128)(2,1)}), bf16[16,24,1536]{2,1,0:T(8,128)(2,1)S(1)}, u32[]{:S(2)}, u32[]{:S(2)}) async-start(bf16[16,24,1536]{2,1,0:T(8,128)(2,1)} %broadcast_in_dim.19), calls=%async_computation.1 | async-start | bytes 2359296 | tf_op jit(solution)/shard_map/all_to_all | solution.py:357
  108.1 3.1 %collective-permute-start.12 = (bf16[2,96,768]{2,1,0:T(8,128)(2,1)}, bf16[2,96,768]{2,1,0:T(8,128)(2,1)S(1)}, u32[]{:S(2)}, u32[]{:S(2)}) collective-permute-start(bf16[2,96,768]{2,1,0:T(8,128)(2,1)} %get-tuple-element.53), channel_id=1, source_target_pairs={{0,32},{32,64},{64,96},{96,128},{128,160},{160,192},{192,224},{1,3... | collective-permute-start | bytes 884744 | tf_op jit(solution)/shard_map/ppermute | solution.py:331
  111.2 4.3 %collective-permute-start.13 = (bf16[2,96,768]{2,1,0:T(8,128)(2,1)}, bf16[2,96,768]{2,1,0:T(8,128)(2,1)}, u32[]{:S(2)}, u32[]{:S(2)}) collective-permute-start(bf16[2,96,768]{2,1,0:T(8,128)(2,1)} %get-tuple-element.54), channel_id=1, source_target_pairs={{32,0},{64,32},{96,64},{128,96},{160,128},{192,160},{224,192},{33,... | collective-permute-start | bytes 884744 | tf_op jit(solution)/shard_map/ppermute | solution.py:331
  115.5 11.3 %collective-permute-done.12.from_north_ref = bf16[2,96,768]{2,1,0:T(8,128)(2,1)S(1)} collective-permute-done((bf16[2,96,768]{2,1,0:T(8,128)(2,1)}, bf16[2,96,768]{2,1,0:T(8,128)(2,1)S(1)}, u32[]{:S(2)}, u32[]{:S(2)}) %collective-permute-start.12) | collective-permute-done | bytes 294944 | tf_op jit(solution)/shard_map/ppermute | solution.py:331
  128.7 4.1 %collective-permute-start.14 = (bf16[384,1536]{1,0:T(8,128)(2,1)S(1)}, bf16[384,1536]{1,0:T(8,128)(2,1)}, u32[]{:S(2)}, u32[]{:S(2)}) collective-permute-start(bf16[384,1536]{1,0:T(8,128)(2,1)S(1)} %bitcast.14), channel_id=1, source_target_pairs={{0,1},{1,0},{2,3},{3,2},{4,5},{5,4},{6,7},{7,6},{8,9},{9,8},{10,11... | collective-permute-start | bytes 3538952 | tf_op jit(solution)/shard_map/ppermute | solution.py:340
  134.6 2.9 %shard_map.170 = (bf16[256,768]{1,0:T(8,128)(2,1)}, bf16[256,768]{1,0:T(8,128)(2,1)}) custom-call(s32[1]{0:T(128)} %bitcast.3.core_ref.which_ref, bf16[2,256,192]{2,1,0:T(8,128)(2,1)} %constant.69.clone.spread_ref, f32[2,256,768]{2,1,0:T(8,128)} %get-tuple-element.42.own_ref, bf16[2,176,768]{2,1,0:T(8,128)(2,1)} %collective-permute-done.8.chip_ref, ...), custom_call_target="tpu_custom_call" | custom-call | flops 1000000000 | bytes 6000000 | tf_op jit(solution)/shard_map/pallas_call | solution.py:114
  137.5 3.3 %shard_map.172 = f32[768,1536]{1,0:T(8,128)} custom-call(s32[1]{0:T(128)S(6)} %sub.31.which_ref, bf16[384,1536]{1,0:T(8,128)(2,1)} %collective-permute-done.14.half_ref, f32[768,1536]{1,0:T(8,128)} %shard_map.171.refs_0_), custom_call_target="tpu_custom_call", output_to_operand_aliasing={{}: (2, {})} | custom-call | flops 1000000 | bytes 4000000 | tf_op jit(solution)/shard_map/pallas_call | solution.py:314
  (57 shorter events, 25.9 us)
Async XLA Ops:
  0.6 57.5 %copy-start = (bf16[768,1536]{1,0:T(8,128)(2,1)S(1)}, bf16[768,1536]{1,0:T(8,128)(2,1)}, u32[]{:S(2)}) copy-start(bf16[768,1536]{1,0:T(8,128)(2,1)} %param.18) | copy-start | bytes 7077892
  0.7 13.2 %copy-start.3 = (s32[2,608]{1,0:T(2,128)S(1)}, s32[2,608]{1,0:T(2,128)}, u32[]{:S(2)}) copy-start(s32[2,608]{1,0:T(2,128)} %constant.66.clone) | copy-start | bytes 14596
  0.7 13.2 %copy-start.4 = (s32[2,608]{1,0:T(2,128)S(1)}, s32[2,608]{1,0:T(2,128)}, u32[]{:S(2)}) copy-start(s32[2,608]{1,0:T(2,128)} %constant.64.clone) | copy-start | bytes 14596
  0.7 13.2 %copy-start.5 = (s32[2,608]{1,0:T(2,128)S(1)}, s32[2,608]{1,0:T(2,128)}, u32[]{:S(2)}) copy-start(s32[2,608]{1,0:T(2,128)} %constant.63.clone) | copy-start | bytes 14596
  3.3 12.1 %collective-permute-start = (bf16[2,96,768]{2,1,0:T(8,128)(2,1)}, bf16[2,96,768]{2,1,0:T(8,128)(2,1)S(1)}, u32[]{:S(2)}, u32[]{:S(2)}) collective-permute-start(bf16[2,96,768]{2,1,0:T(8,128)(2,1)} %get-tuple-element.32), channel_id=1, source_target_pairs={{0,32},{32,64},{64,96},{96,128},{128,160},{160,192},{192,224},{1,3... | collective-permute-start | bytes 884744 | tf_op jit(solution)/shard_map/ppermute | solution.py:331
  6.5 9.9 %collective-permute-start.1 = (bf16[2,96,768]{2,1,0:T(8,128)(2,1)}, bf16[2,96,768]{2,1,0:T(8,128)(2,1)S(1)}, u32[]{:S(2)}, u32[]{:S(2)}) collective-permute-start(bf16[2,96,768]{2,1,0:T(8,128)(2,1)} %get-tuple-element.33), channel_id=1, source_target_pairs={{32,0},{64,32},{96,64},{128,96},{160,128},{192,160},{224,192},{33,... | collective-permute-start | bytes 884744 | tf_op jit(solution)/shard_map/ppermute | solution.py:331
  10.7 16.2 %collective-permute-start.2 = (bf16[2,96,768]{2,1,0:T(8,128)(2,1)}, bf16[2,96,768]{2,1,0:T(8,128)(2,1)S(1)}, u32[]{:S(2)}, u32[]{:S(2)}) collective-permute-start(bf16[2,96,768]{2,1,0:T(8,128)(2,1)} %get-tuple-element.34), channel_id=1, source_target_pairs={{0,1},{1,0},{2,3},{3,2},{4,5},{5,4},{6,7},{7,6},{8,9},{9,8},{10,11... | collective-permute-start | bytes 884744 | tf_op jit(solution)/shard_map/ppermute | solution.py:340
  12.0 14.9 %collective-permute-start.3 = (bf16[2,96,768]{2,1,0:T(8,128)(2,1)}, bf16[2,96,768]{2,1,0:T(8,128)(2,1)}, u32[]{:S(2)}, u32[]{:S(2)}) collective-permute-start(bf16[2,96,768]{2,1,0:T(8,128)(2,1)} %get-tuple-element.35), channel_id=1, source_target_pairs={{0,31},{1,2},{2,1},{3,4},{4,3},{5,6},{6,5},{7,8},{8,7},{9,10},{10,... | collective-permute-start | bytes 884744 | tf_op jit(solution)/shard_map/ppermute | solution.py:336
  13.8 11.8 %copy-start.7 = (s32[2,128]{1,0:T(2,128)S(1)}, s32[2,128]{1,0:T(2,128)}, u32[]{:S(2)}) copy-start(s32[2,128]{1,0:T(2,128)} %constant.65.clone) | copy-start | bytes 3076
  13.9 11.8 %copy-start.6 = (s32[2,128]{1,0:T(2,128)S(1)}, s32[2,128]{1,0:T(2,128)}, u32[]{:S(2)}) copy-start(s32[2,128]{1,0:T(2,128)} %constant.75) | copy-start | bytes 3076
  19.2 7.8 %collective-permute-start.4 = (bf16[2,80,768]{2,1,0:T(8,128)(2,1)}, bf16[2,80,768]{2,1,0:T(8,128)(2,1)S(1)}, u32[]{:S(2)}, u32[]{:S(2)}) collective-permute-start(bf16[2,80,768]{2,1,0:T(8,128)(2,1)} %get-tuple-element.36), channel_id=1, source_target_pairs={{0,1},{1,0},{2,3},{3,2},{4,5},{5,4},{6,7},{7,6},{8,9},{9,8},{10,11... | collective-permute-start | bytes 737288 | tf_op jit(solution)/shard_map/ppermute | solution.py:340
  25.7 10.0 %collective-permute-start.5 = (bf16[2,80,768]{2,1,0:T(8,128)(2,1)}, bf16[2,80,768]{2,1,0:T(8,128)(2,1)S(1)}, u32[]{:S(2)}, u32[]{:S(2)}) collective-permute-start(bf16[2,80,768]{2,1,0:T(8,128)(2,1)} %get-tuple-element.37), channel_id=1, source_target_pairs={{0,31},{1,2},{2,1},{3,4},{4,3},{5,6},{6,5},{7,8},{8,7},{9,10},{10,... | collective-permute-start | bytes 737288 | tf_op jit(solution)/shard_map/ppermute | solution.py:336
  27.0 9.3 %copy-start.12 = (bf16[2,80,768]{2,1,0:T(8,128)(2,1)}, bf16[2,80,768]{2,1,0:T(8,128)(2,1)S(1)}, u32[]{:S(2)}) copy-start(bf16[2,80,768]{2,1,0:T(8,128)(2,1)S(1)} %collective-permute-done.4.refs_4_) | copy-start | bytes 737284
  45.9 3.2 %collective-permute-start.6 = (bf16[384,1536]{1,0:T(8,128)(2,1)}, bf16[384,1536]{1,0:T(8,128)(2,1)}, u32[]{:S(2)}, u32[]{:S(2)}) collective-permute-start(bf16[384,1536]{1,0:T(8,128)(2,1)} %convolution_convert_fusion), channel_id=1, source_target_pairs={{0,1},{1,0},{2,3},{3,2},{4,5},{5,4},{6,7},{7,6},{8,9},{9,8},{10,11... | collective-permute-start | bytes 3538952 | tf_op jit(solution)/shard_map/ppermute | solution.py:340
  51.9 24.3 %all-to-all-start = ((bf16[16,24,1536]{2,1,0:T(8,128)(2,1)}), bf16[16,24,1536]{2,1,0:T(8,128)(2,1)S(1)}, u32[]{:S(2)}, u32[]{:S(2)}) async-start(bf16[16,24,1536]{2,1,0:T(8,128)(2,1)} %bitcast.16), calls=%async_computation | async-start | bytes 2359296 | tf_op jit(solution)/shard_map/all_to_all | solution.py:357
  70.0 12.6 %collective-permute-start.8 = (bf16[2,176,768]{2,1,0:T(8,128)(2,1)}, bf16[2,176,768]{2,1,0:T(8,128)(2,1)}, u32[]{:S(2)}, u32[]{:S(2)}) collective-permute-start(bf16[2,176,768]{2,1,0:T(8,128)(2,1)} %get-tuple-element.44), channel_id=1, source_target_pairs={{0,1},{1,0},{2,3},{3,2},{4,5},{5,4},{6,7},{7,6},{8,9},{9,8},{10,11... | collective-permute-start | bytes 1622024 | tf_op jit(solution)/shard_map/ppermute | solution.py:340
  71.0 16.4 %collective-permute-start.9 = (bf16[2,176,768]{2,1,0:T(8,128)(2,1)}, bf16[2,176,768]{2,1,0:T(8,128)(2,1)}, u32[]{:S(2)}, u32[]{:S(2)}) collective-permute-start(bf16[2,176,768]{2,1,0:T(8,128)(2,1)} %get-tuple-element.45), channel_id=1, source_target_pairs={{0,31},{1,2},{2,1},{3,4},{4,3},{5,6},{6,5},{7,8},{8,7},{9,10},{10,... | collective-permute-start | bytes 1622024 | tf_op jit(solution)/shard_map/ppermute | solution.py:336
  77.0 4.8 %collective-permute-start.7 = (bf16[24,1536]{1,0:T(8,128)(2,1)}, bf16[24,1536]{1,0:T(8,128)(2,1)S(1)}, u32[]{:S(2)}, u32[]{:S(2)}) collective-permute-start(bf16[24,1536]{1,0:T(8,128)(2,1)} %reduce_sum.12), channel_id=1, source_target_pairs={{0,4},{4,0},{8,12},{12,8},{16,20},{20,16},{24,28},{28,24},{1,5},{5... | collective-permute-start | bytes 221192 | tf_op jit(solution)/shard_map/ppermute | solution.py:340
  87.4 4.6 %collective-permute-start.10 = (bf16[24,1536]{1,0:T(8,128)(2,1)S(1)}, bf16[24,1536]{1,0:T(8,128)(2,1)S(1)}, u32[]{:S(2)}, u32[]{:S(2)}) collective-permute-start(bf16[24,1536]{1,0:T(8,128)(2,1)S(1)} %convert_add_fusion.1), channel_id=1, source_target_pairs={{0,8},{4,12},{8,0},{12,4},{16,24},{20,28},{24,16},{28,20},{1,9},{5... | collective-permute-start | bytes 221192 | tf_op jit(solution)/shard_map/ppermute | solution.py:340
  92.1 9.7 %collective-permute-start.11 = (bf16[24,1536]{1,0:T(8,128)(2,1)S(1)}, bf16[24,1536]{1,0:T(8,128)(2,1)S(1)}, u32[]{:S(2)}, u32[]{:S(2)}) collective-permute-start(bf16[24,1536]{1,0:T(8,128)(2,1)S(1)} %add_convert_fusion), channel_id=1, source_target_pairs={{0,16},{4,20},{8,24},{12,28},{16,0},{20,4},{24,8},{28,12},{1,17},{... | collective-permute-start | bytes 221192 | tf_op jit(solution)/shard_map/ppermute | solution.py:340
  102.9 25.7 %all-to-all-start.1 = ((bf16[16,24,1536]{2,1,0:T(8,128)(2,1)}), bf16[16,24,1536]{2,1,0:T(8,128)(2,1)S(1)}, u32[]{:S(2)}, u32[]{:S(2)}) async-start(bf16[16,24,1536]{2,1,0:T(8,128)(2,1)} %broadcast_in_dim.19), calls=%async_computation.1 | async-start | bytes 2359296 | tf_op jit(solution)/shard_map/all_to_all | solution.py:357
  108.1 18.7 %collective-permute-start.12 = (bf16[2,96,768]{2,1,0:T(8,128)(2,1)}, bf16[2,96,768]{2,1,0:T(8,128)(2,1)S(1)}, u32[]{:S(2)}, u32[]{:S(2)}) collective-permute-start(bf16[2,96,768]{2,1,0:T(8,128)(2,1)} %get-tuple-element.53), channel_id=1, source_target_pairs={{0,32},{32,64},{64,96},{96,128},{128,160},{160,192},{192,224},{1,3... | collective-permute-start | bytes 884744 | tf_op jit(solution)/shard_map/ppermute | solution.py:331
  111.2 17.4 %collective-permute-start.13 = (bf16[2,96,768]{2,1,0:T(8,128)(2,1)}, bf16[2,96,768]{2,1,0:T(8,128)(2,1)}, u32[]{:S(2)}, u32[]{:S(2)}) collective-permute-start(bf16[2,96,768]{2,1,0:T(8,128)(2,1)} %get-tuple-element.54), channel_id=1, source_target_pairs={{32,0},{64,32},{96,64},{128,96},{160,128},{192,160},{224,192},{33,... | collective-permute-start | bytes 884744 | tf_op jit(solution)/shard_map/ppermute | solution.py:331
  128.7 8.9 %collective-permute-start.14 = (bf16[384,1536]{1,0:T(8,128)(2,1)S(1)}, bf16[384,1536]{1,0:T(8,128)(2,1)}, u32[]{:S(2)}, u32[]{:S(2)}) collective-permute-start(bf16[384,1536]{1,0:T(8,128)(2,1)S(1)} %bitcast.14), channel_id=1, source_target_pairs={{0,1},{1,0},{2,3},{3,2},{4,5},{5,4},{6,7},{7,6},{8,9},{9,8},{10,11... | collective-permute-start | bytes 3538952 | tf_op jit(solution)/shard_map/ppermute | solution.py:340
  (7 other events, 24.7 us)

commit v3 on v2

--- a/solution.py
+++ b/solution.py
@@ -164,7 +164,7 @@
     return jnp.concatenate(mid + [chip, chip_corner[corner], beyond, beyond_corner[corner]], axis=0)
 
 
-def forward_kernel(q_ref, k_ref, v_ref, *refs):
+def forward_kernel(base_ref, q_ref, k_ref, v_ref, *refs):
     halo_refs, (bias_ref, out_ref, lse_ref) = refs[:HALOS], refs[HALOS:]
     keys = (k_ref[...], *(ref[0] for ref in halo_refs))
     values = (v_ref[...], *(ref[1] for ref in halo_refs))
@@ -179,7 +179,7 @@
         lse_ref[0, tile : tile + 1, :] = top + jnp.log(total)
 
 
-def backward_kernel(q_ref, k_ref, v_ref, *refs):
+def backward_kernel(shift_ref, q_ref, k_ref, v_ref, *refs):
     halo_refs, (bias_ref, g_ref, lse_ref) = refs[:HALOS], refs[HALOS : HALOS + 3]
     dq_ref, own_ref, poles_ref, dchip_ref, dnext_ref, prob_s, score_s = refs[HALOS + 3 :]
 
@@ -220,39 +220,47 @@
     return pl.BlockSpec(shape, lambda h, *at: (0,) * (len(lead) + 1) + (h,))
 
 
-def input_specs():
-    tokens = by_heads((), TOKENS)
-    halos = [by_heads((2,), EDGE)] * 4 + [by_heads((2,), CORNER)] * 2
-    bias = pl.BlockSpec((TILES, KEYS, TILE_Q), lambda h: (0, 0, 0))
+def from_head(lead, rows):
+    return pl.BlockSpec(lead + (rows, HEAD_DIM), lambda h, at: (0,) * (len(lead) + 1) + (at[0] + h,))
+
+
+def input_specs(head_spec):
+    tokens = head_spec((), TOKENS)
+    halos = [head_spec((2,), EDGE)] * 4 + [head_spec((2,), CORNER)] * 2
+    bias = pl.BlockSpec((TILES, KEYS, TILE_Q), lambda h, *at: (0, 0, 0))
     return [tokens] * 3 + halos + [bias]
 
 
-def lse_spec():
-    return pl.BlockSpec((1, 8, TILE_Q), lambda h: (h, 0, 0))
-
-
-def forward_attention(q, k, v, halos, bias):
+def forward_attention(base, q, k, v, halos, bias):
     return pl.pallas_call(
         forward_kernel,
-        grid=(HEADS,),
-        in_specs=input_specs(),
-        out_specs=[by_heads((), TOKENS), lse_spec()],
+        grid_spec=pltpu.PrefetchScalarGridSpec(
+            num_scalar_prefetch=1,
+            grid=(HALF_HEADS,),
+            in_specs=input_specs(from_head),
+            out_specs=[by_heads((), TOKENS), pl.BlockSpec((1, 8, TILE_Q), lambda h, at: (h, 0, 0))],
+        ),
         out_shape=[
-            jax.ShapeDtypeStruct((TOKENS, CHANNELS), BF16),
-            jax.ShapeDtypeStruct((HEADS, 8, TILE_Q), F32),
+            jax.ShapeDtypeStruct((TOKENS, HALF), BF16),
+            jax.ShapeDtypeStruct((HALF_HEADS, 8, TILE_Q), F32),
         ],
         compiler_params=FULL,
         cost_estimate=pl.CostEstimate(flops=2 * 10**9, bytes_accessed=6 * 10**6, transcendentals=10**6),
-    )(q, k, v, *halos, bias)
-
-
-def backward_attention(q, k, v, halos, bias, g, lse):
+    )(base, q, k, v, *halos, bias)
+
+
+def backward_attention(shift, q, k, v, halos, bias, g, lse):
     keys = MID + 2 * SIDE
+    lse_spec = pl.BlockSpec((1, 8, TILE_Q), lambda h, at: (lax.rem(h + at[0], HEADS), 0, 0))
     return pl.pallas_call(
         backward_kernel,
-        grid=(HEADS,),
-        in_specs=input_specs() + [by_heads((), TOKENS), lse_spec()],
-        out_specs=[by_heads((), TOKENS)] + [by_heads((2,), rows) for rows in (TOKENS, 2 * EDGE, SIDE, SIDE)],
+        grid_spec=pltpu.PrefetchScalarGridSpec(
+            num_scalar_prefetch=1,
+            grid=(HEADS,),
+            in_specs=input_specs(by_heads) + [by_heads((), TOKENS), lse_spec],
+            out_specs=[by_heads((), TOKENS)] + [by_heads((2,), rows) for rows in (TOKENS, 2 * EDGE, SIDE, SIDE)],
+            scratch_shapes=[pltpu.VMEM((keys, TOKENS), BF16), pltpu.VMEM((keys, TOKENS), BF16)],
+        ),
         out_shape=[
             jax.ShapeDtypeStruct((TOKENS, CHANNELS), BF16),
             jax.ShapeDtypeStruct((2, TOKENS, CHANNELS), F32),
@@ -260,10 +268,9 @@
             jax.ShapeDtypeStruct((2, SIDE, CHANNELS), BF16),
             jax.ShapeDtypeStruct((2, SIDE, CHANNELS), BF16),
         ],
-        scratch_shapes=[pltpu.VMEM((keys, TOKENS), BF16), pltpu.VMEM((keys, TOKENS), BF16)],
         compiler_params=FULL,
         cost_estimate=pl.CostEstimate(flops=6 * 10**9, bytes_accessed=12 * 10**6, transcendentals=10**6),
-    )(q, k, v, *halos, bias, g, lse)
+    )(shift, q, k, v, *halos, bias, g, lse)
 
 
 def merge_poles_kernel(core_ref, spread_ref, poles_ref, chip_ref, next_ref, north_ref, south_ref):
@@ -370,33 +377,32 @@
     bias = window_bias(core, lax.axis_index(LAT) * ROWS, ROWS * lax.axis_size(LAT))
     grad_attn = dot(grad_rows, out_weight, ((1,), (1,))).astype(BF16)
 
-    attended, lse = forward_attention(q, k, v, halos, bias)
-
-    def term(half):
-        return dot(lax.dynamic_slice_in_dim(attended, half * HALF, HALF, axis=1), grad_rows, ((0,), (0,)))
-
-    received = swapped(term(1 - core).astype(BF16), "core", 1)
-    pieces = plane_sum((term(core) + received.astype(F32)).astype(BF16))
-    grad_q, own, poles, side_chip, side_next = backward_attention(q, k, v, halos, bias, grad_attn, lse)
+    theirs, lse_theirs = forward_attention(HALF_HEADS * (1 - which), q, k, v, halos, bias)
+    received = with_chip(dot(theirs, grad_rows, ((0,), (0,))).astype(BF16))
+    mine, lse_mine = forward_attention(HALF_HEADS * which, q, k, v, halos, bias)
+    pieces = plane_sum((dot(mine, grad_rows, ((0,), (0,))) + received.astype(F32)).astype(BF16))
+    grad_q, own, poles, side_chip, side_next = backward_attention(
+        HALF_HEADS * (1 - which), q, k, v, halos, bias, grad_attn,
+        jnp.concatenate([lse_theirs, lse_mine], axis=0),
+    )
     from_chip, from_next = with_chip(side_chip), with_next_chip(side_next)
-
-    def z_step(total, bit):
-        part = total.astype(BF16)
-        return part.astype(F32) + swapped(part, "z", bit).astype(F32)
 
     pieces, grad_q = lax.optimization_barrier((pieces, grad_q))
     total = jnp.sum(pieces.astype(F32), axis=0)
-    total = z_step(total, 1)
+    part = total.astype(BF16)
+    near, far, last = (swapped(part, "z", bit).astype(F32) for bit in (1, 2, 3))
+    total = (part.astype(F32) + near) + (far + last)
     total, from_chip, from_next = lax.optimization_barrier((total, from_chip, from_next))
     north, south = merge_poles(which, poles, from_chip, from_next)
-    total = z_step(z_step(total, 2), 4)
+    part = total.astype(BF16)
+    total = part.astype(F32) + swapped(part, "z", 4).astype(F32)
     total, north, south = lax.optimization_barrier((total, north, south))
     group = lax.axis_size(PLANE)
     part = jnp.broadcast_to(total.astype(BF16)[None], (group, HALF // group, WIDTH))
     whole = plane_sum(part).reshape(HALF, WIDTH)
     from_north, from_south = along_lat(south, 1), along_lat(north, -1)
-    whole, from_north, from_south = lax.optimization_barrier((whole, from_north, from_south))
     grad_k, grad_v = merge_own(which, own, from_chip, from_next, from_north, from_south)
+    whole, grad_k, grad_v = lax.optimization_barrier((whole, grad_k, grad_v))
     other = swapped(whole, "core", 1)
     grad_weight = widen_half(whole, which)
     grad_weight = widen_half(other, 1 - which, grad_weight)

time: 142 us -> 136 us (0.958)
  waiting for transfers between devices: 39.6 us -> 35.2 us
  starting transfers between devices: 54.6 us -> 52.4 us
    ppermute x3, waiting for transfers between devices: 13.4 us -> 9.4 us  [with_next_chip(): lax.ppermute(block, LON, [(j, (j + 2 * (j % 2) - 1) % strips) for j in ra...]
    ppermute x8 -> x9, starting transfers between devices: 24.8 us -> 21.7 us  [swapped(): lax.ppermute(block, axis, [(i, i ^ bit) for i in range(lax.axis_size(axis...]
    pallas_call x2 -> x3, Pallas kernels: 16.3 us -> 18.5 us  [the longest x1 9.31 us: backward_attention(): pl.pallas_call(backward_kernel, grid_spec=pltpu.PrefetchScalarGridSpec(nu...]
    ppermute x8 -> x9, waiting for transfers between devices: 7.96 us -> 6.17 us  [swapped(): lax.ppermute(block, axis, [(i, i ^ bit) for i in range(lax.axis_size(axis...]
    ppermute x4, waiting for transfers between devices: 14.9 us -> 16.5 us  [along_lat(): lax.ppermute(block, LAT, [(i, i + by) for i in range(bands) if 0 <= i + b...]
    pallas_call x2, Pallas kernels: 5.17 us -> 3.72 us  [widen_half(): pl.pallas_call(widen_kernel, grid_spec=pltpu.PrefetchScalarGridSpec(num_s...]
  transfers between devices with their start and end apart: 17 -> 18, of which waited for: 11 -> 11; matrix products, arithmetic and copies ran while one was open for 4% -> 5% of each run, Pallas kernels for 13% -> 17%
where the time goes in v3:
time: 136 us; the launch traced here: 135 us
  starting transfers between devices  52.4 us (39%)
  waiting for transfers between devices  35.2 us (26%)
  Pallas kernels  32.3 us (24%)
  matrix products  8.05 us (6%)
  other arithmetic  3.58 us (3%)
  local copies, waits for them, and re-layouts  2.59 us (2%)
    ppermute x9, starting transfers between devices, swapped(): lax.ppermute(block, axis, [(i, i ^ bit) for i in range(lax.axis_size(axis...  21.7 us
    ppermute x4, waiting for transfers between devices, along_lat(): lax.ppermute(block, LAT, [(i, i + by) for i in range(bands) if 0 <= i + b...  16.5 us
    ppermute x4, starting transfers between devices, along_lat(): lax.ppermute(block, LAT, [(i, i + by) for i in range(bands) if 0 <= i + b...  14.8 us
    all_to_all x2, starting transfers between devices, plane_sum(): lax.all_to_all(pair.reshape(group, HALF // group, WIDTH), PLANE, split_ax...  12.3 us
    pallas_call x4, Pallas kernels, with_picks(): pl.pallas_call(kernel, grid_spec=pltpu.PrefetchScalarGridSpec(num_scalar_...  10.2 us
    ppermute x3, waiting for transfers between devices, with_next_chip(): lax.ppermute(block, LON, [(j, (j + 2 * (j % 2) - 1) % strips) for j in ra...  9.4 us
    pallas_call x1, Pallas kernels, backward_attention(): pl.pallas_call(backward_kernel, grid_spec=pltpu.PrefetchScalarGridSpec(nu...  9.31 us
    pallas_call x2, Pallas kernels, forward_attention(): pl.pallas_call(forward_kernel, grid_spec=pltpu.PrefetchScalarGridSpec(num...  9.15 us
  transfers between devices with their start and end apart: 18, of which 11 were waited for; matrix products, arithmetic and copies ran while one was open for 5% of the time, Pallas kernels for 17%

profile of v3, /device:TPU:3, one launch (start us, length us, event | category | flops | bytes accessed | tf_op | source)
XLA Modules:
  0.0 135.0 jit_solution(2657486978134124732)
XLA Ops:
  0.7 2.6 %shard_map.165 = (bf16[2,96,768]{2,1,0:T(8,128)(2,1)}, bf16[2,96,768]{2,1,0:T(8,128)(2,1)}, bf16[2,96,768]{2,1,0:T(8,128)(2,1)}, bf16[2,96,768]{2,1,0:T(8,128)(2,1)}) custom-call(s32[1]{0:T(128)} %bitcast.core_ref.which_ref, bf16[2,192,256]{2,1,0:T(8,128)(2,1)} %constant.57.clone.picks_ref, bf16[256,768]{1,0:T(8,128)(2,1)} %bitcast.24, bf16[256,768]{1,0:T(8,128)(2,1)} %bitcast.28), custom_call_target="tpu_custom_call" | custom-call | flops 1000000000 | bytes 2000000 | tf_op jit(solution)/shard_map/pallas_call | solution.py:114
  3.3 3.2 %collective-permute-start = (bf16[2,96,768]{2,1,0:T(8,128)(2,1)}, bf16[2,96,768]{2,1,0:T(8,128)(2,1)S(1)}, u32[]{:S(2)}, u32[]{:S(2)}) collective-permute-start(bf16[2,96,768]{2,1,0:T(8,128)(2,1)} %get-tuple-element.34), channel_id=1, source_target_pairs={{0,32},{32,64},{64,96},{96,128},{128,160},{160,192},{192,224},{1,3... | collective-permute-start | bytes 884744 | tf_op jit(solution)/shard_map/ppermute | solution.py:338
  6.5 4.2 %collective-permute-start.1 = (bf16[2,96,768]{2,1,0:T(8,128)(2,1)}, bf16[2,96,768]{2,1,0:T(8,128)(2,1)S(1)}, u32[]{:S(2)}, u32[]{:S(2)}) collective-permute-start(bf16[2,96,768]{2,1,0:T(8,128)(2,1)} %get-tuple-element.35), channel_id=1, source_target_pairs={{32,0},{64,32},{96,64},{128,96},{160,128},{192,160},{224,192},{33,... | collective-permute-start | bytes 884744 | tf_op jit(solution)/shard_map/ppermute | solution.py:338
  19.2 6.5 %collective-permute-start.4 = (bf16[2,80,768]{2,1,0:T(8,128)(2,1)}, bf16[2,80,768]{2,1,0:T(8,128)(2,1)S(1)}, u32[]{:S(2)}, u32[]{:S(2)}) collective-permute-start(bf16[2,80,768]{2,1,0:T(8,128)(2,1)} %get-tuple-element.38), channel_id=1, source_target_pairs={{0,1},{1,0},{2,3},{3,2},{4,5},{5,4},{6,7},{7,6},{8,9},{9,8},{10,11... | collective-permute-start | bytes 737288 | tf_op jit(solution)/shard_map/ppermute | solution.py:347
  27.0 8.6 %collective-permute-done.5.refs_5_ = bf16[2,80,768]{2,1,0:T(8,128)(2,1)S(1)} collective-permute-done((bf16[2,80,768]{2,1,0:T(8,128)(2,1)}, bf16[2,80,768]{2,1,0:T(8,128)(2,1)S(1)}, u32[]{:S(2)}, u32[]{:S(2)}) %collective-permute-start.5) | collective-permute-done | bytes 245792 | tf_op jit(solution)/shard_map/ppermute | solution.py:343
  36.3 4.6 %shard_map.168 = (bf16[256,384]{1,0:T(8,128)(2,1)}, f32[3,8,128]{2,1,0:T(8,128)}) custom-call(s32[1]{0:T(128)S(6)} %mul.16.base_ref.shift_ref, bf16[256,768]{1,0:T(8,128)(2,1)} %bitcast.21, bf16[256,768]{1,0:T(8,128)(2,1)} %bitcast.25, bf16[256,768]{1,0:T(8,128)(2,1)} %bitcast.29, bf16[2,96,768]{2,1,0:T(8,128)(2,1)} %copy-done.9, ...), custom_call_target="tpu_custom_call" | custom-call | flops 2000000000 | bytes 6000000 | tf_op jit(solution)/shard_map/pallas_call | solution.py:235
  40.9 2.4 %convolution_convert_fusion = bf16[384,1536]{1,0:T(8,128)(2,1)} fusion(bf16[256,384]{1,0:T(8,128)(2,1)} %get-tuple-element.41, bf16[256,1536]{1,0:T(8,128)(2,1)S(1)} %bitcast.19), kind=kOutput, calls=%fused_computation.2 | convolution fusion | flops 302579712 | bytes 2162688 | tf_op jit(solution)/shard_map/dot_general | solution.py:108
  43.7 4.6 %shard_map.167 = (bf16[256,384]{1,0:T(8,128)(2,1)}, f32[3,8,128]{2,1,0:T(8,128)}) custom-call(s32[1]{0:T(128)S(6)} %mul.13.base_ref, bf16[256,768]{1,0:T(8,128)(2,1)} %bitcast.22, bf16[256,768]{1,0:T(8,128)(2,1)} %bitcast.26, bf16[256,768]{1,0:T(8,128)(2,1)} %bitcast.30, bf16[2,96,768]{2,1,0:T(8,128)(2,1)} %copy-done.9, bf16[2,96,768]{2,1,0:T(8,128)(2,1)} %copy-done.10, ...), custom_call_target="tpu_custom_call" | custom-call | flops 2000000000 | bytes 6000000 | tf_op jit(solution)/shard_map/pallas_call | solution.py:235
  48.2 2.9 %fusion = bf16[384,1536]{1,0:T(8,128)(2,1)} fusion(bf16[256,384]{1,0:T(8,128)(2,1)} %get-tuple-element.40, bf16[256,1536]{1,0:T(8,128)(2,1)S(1)} %bitcast.20, bf16[384,1536]{1,0:T(8,128)(2,1)} %collective-permute-done.6), kind=kOutput, calls=%fused_computation.1 | convolution fusion | flops 303759360 | bytes 3342336 | tf_op jit(solution)/shard_map/dot_general | solution.py:108
  51.1 6.3 %all-to-all-start = ((bf16[16,24,1536]{2,1,0:T(8,128)(2,1)}), bf16[16,24,1536]{2,1,0:T(8,128)(2,1)S(1)}, u32[]{:S(2)}, u32[]{:S(2)}) async-start(bf16[16,24,1536]{2,1,0:T(8,128)(2,1)} %bitcast.5), calls=%async_computation | async-start | bytes 2359296 | tf_op jit(solution)/shard_map/all_to_all | solution.py:364
  57.5 2.7 %convolution_convert_fusion.1.refs_7_ = bf16[256,768]{1,0:T(8,128)(2,1)} fusion(bf16[256,1536]{1,0:T(8,128)(2,1)} %bitcast.18, bf16[768,1536]{1,0:T(8,128)(2,1)S(1)} %copy-done), kind=kOutput, calls=%fused_computation.3 | convolution fusion | flops 604176384 | bytes 3538944 | tf_op jit(solution)/shard_map/dot_general | solution.py:108
  60.8 9.3 %shard_map.169 = (bf16[256,768]{1,0:T(8,128)(2,1)}, f32[2,256,768]{2,1,0:T(8,128)}, f32[2,192,768]{2,1,0:T(8,128)}, bf16[2,176,768]{2,1,0:T(8,128)(2,1)}, bf16[2,176,768]{2,1,0:T(8,128)(2,1)}) custom-call(s32[1]{0:T(128)S(6)} %mul.16.base_ref.shift_ref, bf16[256,768]{1,0:T(8,128)(2,1)} %bitcast.23, bf16[256,768]{1,0:T(8,128)(2,1)} %bitcast.27, ...), custom_call_target="tpu_custom_call" | custom-call | flops 6000000000 | bytes 12000000 | tf_op jit(solution)/shard_map/pallas_call | solution.py:255
  72.5 3.2 %all-to-all-done = bf16[16,24,1536]{2,1,0:T(8,128)(2,1)S(1)} async-done(((bf16[16,24,1536]{2,1,0:T(8,128)(2,1)}), bf16[16,24,1536]{2,1,0:T(8,128)(2,1)S(1)}, u32[]{:S(2)}, u32[]{:S(2)}) %all-to-all-start) | async-done | bytes 1179680 | tf_op jit(solution)/shard_map/all_to_all | solution.py:364
  76.4 3.4 %collective-permute-start.9 = (bf16[24,1536]{1,0:T(8,128)(2,1)}, bf16[24,1536]{1,0:T(8,128)(2,1)S(1)}, u32[]{:S(2)}, u32[]{:S(2)}) collective-permute-start(bf16[24,1536]{1,0:T(8,128)(2,1)} %reduce_sum.12), channel_id=1, source_target_pairs={{0,12},{4,8},{8,4},{12,0},{16,28},{20,24},{24,20},{28,16},{1,13},{... | collective-permute-start | bytes 221192 | tf_op jit(solution)/shard_map/ppermute | solution.py:347
  80.1 2.9 %collective-permute-done.9 = bf16[24,1536]{1,0:T(8,128)(2,1)S(1)} collective-permute-done((bf16[24,1536]{1,0:T(8,128)(2,1)}, bf16[24,1536]{1,0:T(8,128)(2,1)S(1)}, u32[]{:S(2)}, u32[]{:S(2)}) %collective-permute-start.9) | collective-permute-done | bytes 73760 | tf_op jit(solution)/shard_map/ppermute | solution.py:347
  83.0 2.5 %collective-permute-done.8 = bf16[24,1536]{1,0:T(8,128)(2,1)S(1)} collective-permute-done((bf16[24,1536]{1,0:T(8,128)(2,1)}, bf16[24,1536]{1,0:T(8,128)(2,1)S(1)}, u32[]{:S(2)}, u32[]{:S(2)}) %collective-permute-start.8) | collective-permute-done | bytes 73760 | tf_op jit(solution)/shard_map/ppermute | solution.py:347
  87.3 6.6 %collective-permute-start.12 = (bf16[24,1536]{1,0:T(8,128)(2,1)S(1)}, bf16[24,1536]{1,0:T(8,128)(2,1)S(1)}, u32[]{:S(2)}, u32[]{:S(2)}) collective-permute-start(bf16[24,1536]{1,0:T(8,128)(2,1)S(1)} %add_add_fusion), channel_id=1, source_target_pairs={{0,16},{4,20},{8,24},{12,28},{16,0},{20,4},{24,8},{28,12},{1,17},{... | collective-permute-start | bytes 221192 | tf_op jit(solution)/shard_map/ppermute | solution.py:347
  93.9 2.5 %shard_map.170 = (bf16[2,96,768]{2,1,0:T(8,128)(2,1)}, bf16[2,96,768]{2,1,0:T(8,128)(2,1)}) custom-call(s32[1]{0:T(128)} %bitcast.core_ref.which_ref, bf16[2,192,160]{2,1,0:T(8,128)(2,1)} %constant.64.clone.spread_ref, f32[2,192,768]{2,1,0:T(8,128)} %get-tuple-element.50.poles_ref, bf16[2,176,768]{2,1,0:T(8,128)(2,1)} %collective-permute-done.10.chip_ref, ...), custom_call_target="tpu_custom_call" | custom-call | flops 1000000000 | bytes 4000000 | tf_op jit(solution)/shard_map/pallas_call | solution.py:114
  97.6 6.0 %all-to-all-start.1 = ((bf16[16,24,1536]{2,1,0:T(8,128)(2,1)}), bf16[16,24,1536]{2,1,0:T(8,128)(2,1)S(1)}, u32[]{:S(2)}, u32[]{:S(2)}) async-start(bf16[16,24,1536]{2,1,0:T(8,128)(2,1)} %broadcast_in_dim.19), calls=%async_computation.1 | async-start | bytes 2359296 | tf_op jit(solution)/shard_map/all_to_all | solution.py:364
  103.7 3.1 %collective-permute-start.13 = (bf16[2,96,768]{2,1,0:T(8,128)(2,1)}, bf16[2,96,768]{2,1,0:T(8,128)(2,1)S(1)}, u32[]{:S(2)}, u32[]{:S(2)}) collective-permute-start(bf16[2,96,768]{2,1,0:T(8,128)(2,1)} %get-tuple-element.57), channel_id=1, source_target_pairs={{0,32},{32,64},{64,96},{96,128},{128,160},{160,192},{192,224},{1,3... | collective-permute-start | bytes 884744 | tf_op jit(solution)/shard_map/ppermute | solution.py:338
  106.8 4.3 %collective-permute-start.14 = (bf16[2,96,768]{2,1,0:T(8,128)(2,1)}, bf16[2,96,768]{2,1,0:T(8,128)(2,1)}, u32[]{:S(2)}, u32[]{:S(2)}) collective-permute-start(bf16[2,96,768]{2,1,0:T(8,128)(2,1)} %get-tuple-element.58), channel_id=1, source_target_pairs={{32,0},{64,32},{96,64},{128,96},{160,128},{192,160},{224,192},{33,... | collective-permute-start | bytes 884744 | tf_op jit(solution)/shard_map/ppermute | solution.py:338
  111.1 12.2 %collective-permute-done.13.from_north_ref = bf16[2,96,768]{2,1,0:T(8,128)(2,1)S(1)} collective-permute-done((bf16[2,96,768]{2,1,0:T(8,128)(2,1)}, bf16[2,96,768]{2,1,0:T(8,128)(2,1)S(1)}, u32[]{:S(2)}, u32[]{:S(2)}) %collective-permute-start.13) | collective-permute-done | bytes 294944 | tf_op jit(solution)/shard_map/ppermute | solution.py:338
  125.1 2.9 %shard_map.171 = (bf16[256,768]{1,0:T(8,128)(2,1)}, bf16[256,768]{1,0:T(8,128)(2,1)}) custom-call(s32[1]{0:T(128)} %bitcast.core_ref.which_ref, bf16[2,256,192]{2,1,0:T(8,128)(2,1)} %constant.65.clone.spread_ref, f32[2,256,768]{2,1,0:T(8,128)} %get-tuple-element.56.own_ref, bf16[2,176,768]{2,1,0:T(8,128)(2,1)} %collective-permute-done.10.chip_ref, ...), custom_call_target="tpu_custom_call" | custom-call | flops 1000000000 | bytes 6000000 | tf_op jit(solution)/shard_map/pallas_call | solution.py:114
  128.0 2.7 %collective-permute-start.15 = (bf16[384,1536]{1,0:T(8,128)(2,1)S(1)}, bf16[384,1536]{1,0:T(8,128)(2,1)S(1)}, u32[]{:S(2)}, u32[]{:S(2)}) collective-permute-start(bf16[384,1536]{1,0:T(8,128)(2,1)S(1)} %bitcast.16), channel_id=1, source_target_pairs={{0,1},{1,0},{2,3},{3,2},{4,5},{5,4},{6,7},{7,6},{8,9},{9,8},{10,11... | collective-permute-start | bytes 3538952 | tf_op jit(solution)/shard_map/ppermute | solution.py:347
  (62 shorter events, 24.0 us)
Async XLA Ops:
  0.6 56.8 %copy-start = (bf16[768,1536]{1,0:T(8,128)(2,1)S(1)}, bf16[768,1536]{1,0:T(8,128)(2,1)}, u32[]{:S(2)}) copy-start(bf16[768,1536]{1,0:T(8,128)(2,1)} %param.18) | copy-start | bytes 7077892
  0.7 13.2 %copy-start.4 = (s32[2,608]{1,0:T(2,128)S(1)}, s32[2,608]{1,0:T(2,128)}, u32[]{:S(2)}) copy-start(s32[2,608]{1,0:T(2,128)} %constant.62.clone) | copy-start | bytes 14596
  0.7 13.2 %copy-start.5 = (s32[2,608]{1,0:T(2,128)S(1)}, s32[2,608]{1,0:T(2,128)}, u32[]{:S(2)}) copy-start(s32[2,608]{1,0:T(2,128)} %constant.60.clone) | copy-start | bytes 14596
  0.7 13.2 %copy-start.6 = (s32[2,608]{1,0:T(2,128)S(1)}, s32[2,608]{1,0:T(2,128)}, u32[]{:S(2)}) copy-start(s32[2,608]{1,0:T(2,128)} %constant.59.clone) | copy-start | bytes 14596
  3.3 12.1 %collective-permute-start = (bf16[2,96,768]{2,1,0:T(8,128)(2,1)}, bf16[2,96,768]{2,1,0:T(8,128)(2,1)S(1)}, u32[]{:S(2)}, u32[]{:S(2)}) collective-permute-start(bf16[2,96,768]{2,1,0:T(8,128)(2,1)} %get-tuple-element.34), channel_id=1, source_target_pairs={{0,32},{32,64},{64,96},{96,128},{128,160},{160,192},{192,224},{1,3... | collective-permute-start | bytes 884744 | tf_op jit(solution)/shard_map/ppermute | solution.py:338
  6.5 9.9 %collective-permute-start.1 = (bf16[2,96,768]{2,1,0:T(8,128)(2,1)}, bf16[2,96,768]{2,1,0:T(8,128)(2,1)S(1)}, u32[]{:S(2)}, u32[]{:S(2)}) collective-permute-start(bf16[2,96,768]{2,1,0:T(8,128)(2,1)} %get-tuple-element.35), channel_id=1, source_target_pairs={{32,0},{64,32},{96,64},{128,96},{160,128},{192,160},{224,192},{33,... | collective-permute-start | bytes 884744 | tf_op jit(solution)/shard_map/ppermute | solution.py:338
  10.7 16.2 %collective-permute-start.2 = (bf16[2,96,768]{2,1,0:T(8,128)(2,1)}, bf16[2,96,768]{2,1,0:T(8,128)(2,1)S(1)}, u32[]{:S(2)}, u32[]{:S(2)}) collective-permute-start(bf16[2,96,768]{2,1,0:T(8,128)(2,1)} %get-tuple-element.36), channel_id=1, source_target_pairs={{0,1},{1,0},{2,3},{3,2},{4,5},{5,4},{6,7},{7,6},{8,9},{9,8},{10,11... | collective-permute-start | bytes 884744 | tf_op jit(solution)/shard_map/ppermute | solution.py:347
  12.0 14.9 %collective-permute-start.3 = (bf16[2,96,768]{2,1,0:T(8,128)(2,1)}, bf16[2,96,768]{2,1,0:T(8,128)(2,1)}, u32[]{:S(2)}, u32[]{:S(2)}) collective-permute-start(bf16[2,96,768]{2,1,0:T(8,128)(2,1)} %get-tuple-element.37), channel_id=1, source_target_pairs={{0,31},{1,2},{2,1},{3,4},{4,3},{5,6},{6,5},{7,8},{8,7},{9,10},{10,... | collective-permute-start | bytes 884744 | tf_op jit(solution)/shard_map/ppermute | solution.py:343
  13.8 11.8 %copy-start.8 = (s32[2,128]{1,0:T(2,128)S(1)}, s32[2,128]{1,0:T(2,128)}, u32[]{:S(2)}) copy-start(s32[2,128]{1,0:T(2,128)} %constant.61.clone) | copy-start | bytes 3076
  13.9 11.8 %copy-start.7 = (s32[2,128]{1,0:T(2,128)S(1)}, s32[2,128]{1,0:T(2,128)}, u32[]{:S(2)}) copy-start(s32[2,128]{1,0:T(2,128)} %constant.71) | copy-start | bytes 3076
  19.2 7.8 %collective-permute-start.4 = (bf16[2,80,768]{2,1,0:T(8,128)(2,1)}, bf16[2,80,768]{2,1,0:T(8,128)(2,1)S(1)}, u32[]{:S(2)}, u32[]{:S(2)}) collective-permute-start(bf16[2,80,768]{2,1,0:T(8,128)(2,1)} %get-tuple-element.38), channel_id=1, source_target_pairs={{0,1},{1,0},{2,3},{3,2},{4,5},{5,4},{6,7},{7,6},{8,9},{9,8},{10,11... | collective-permute-start | bytes 737288 | tf_op jit(solution)/shard_map/ppermute | solution.py:347
  25.7 10.0 %collective-permute-start.5 = (bf16[2,80,768]{2,1,0:T(8,128)(2,1)}, bf16[2,80,768]{2,1,0:T(8,128)(2,1)S(1)}, u32[]{:S(2)}, u32[]{:S(2)}) collective-permute-start(bf16[2,80,768]{2,1,0:T(8,128)(2,1)} %get-tuple-element.39), channel_id=1, source_target_pairs={{0,31},{1,2},{2,1},{3,4},{4,3},{5,6},{6,5},{7,8},{8,7},{9,10},{10,... | collective-permute-start | bytes 737288 | tf_op jit(solution)/shard_map/ppermute | solution.py:343
  43.4 4.8 %collective-permute-start.6 = (bf16[384,1536]{1,0:T(8,128)(2,1)}, bf16[384,1536]{1,0:T(8,128)(2,1)}, u32[]{:S(2)}, u32[]{:S(2)}) collective-permute-start(bf16[384,1536]{1,0:T(8,128)(2,1)} %convolution_convert_fusion), channel_id=1, source_target_pairs={{0,1},{1,0},{2,3},{3,2},{4,5},{5,4},{6,7},{7,6},{8,9},{9,8},{10,11... | collective-permute-start | bytes 3538952 | tf_op jit(solution)/shard_map/ppermute | solution.py:347
  51.1 24.5 %all-to-all-start = ((bf16[16,24,1536]{2,1,0:T(8,128)(2,1)}), bf16[16,24,1536]{2,1,0:T(8,128)(2,1)S(1)}, u32[]{:S(2)}, u32[]{:S(2)}) async-start(bf16[16,24,1536]{2,1,0:T(8,128)(2,1)} %bitcast.5), calls=%async_computation | async-start | bytes 2359296 | tf_op jit(solution)/shard_map/all_to_all | solution.py:364
  70.1 16.4 %collective-permute-start.10 = (bf16[2,176,768]{2,1,0:T(8,128)(2,1)}, bf16[2,176,768]{2,1,0:T(8,128)(2,1)}, u32[]{:S(2)}, u32[]{:S(2)}) collective-permute-start(bf16[2,176,768]{2,1,0:T(8,128)(2,1)} %get-tuple-element.47), channel_id=1, source_target_pairs={{0,1},{1,0},{2,3},{3,2},{4,5},{5,4},{6,7},{7,6},{8,9},{9,8},{10,11... | collective-permute-start | bytes 1622024 | tf_op jit(solution)/shard_map/ppermute | solution.py:347
  70.7 16.6 %collective-permute-start.11 = (bf16[2,176,768]{2,1,0:T(8,128)(2,1)}, bf16[2,176,768]{2,1,0:T(8,128)(2,1)}, u32[]{:S(2)}, u32[]{:S(2)}) collective-permute-start(bf16[2,176,768]{2,1,0:T(8,128)(2,1)} %get-tuple-element.48), channel_id=1, source_target_pairs={{0,31},{1,2},{2,1},{3,4},{4,3},{5,6},{6,5},{7,8},{8,7},{9,10},{10,... | collective-permute-start | bytes 1622024 | tf_op jit(solution)/shard_map/ppermute | solution.py:343
  76.4 6.6 %collective-permute-start.9 = (bf16[24,1536]{1,0:T(8,128)(2,1)}, bf16[24,1536]{1,0:T(8,128)(2,1)S(1)}, u32[]{:S(2)}, u32[]{:S(2)}) collective-permute-start(bf16[24,1536]{1,0:T(8,128)(2,1)} %reduce_sum.12), channel_id=1, source_target_pairs={{0,12},{4,8},{8,4},{12,0},{16,28},{20,24},{24,20},{28,16},{1,13},{... | collective-permute-start | bytes 221192 | tf_op jit(solution)/shard_map/ppermute | solution.py:347
  79.8 5.7 %collective-permute-start.8 = (bf16[24,1536]{1,0:T(8,128)(2,1)}, bf16[24,1536]{1,0:T(8,128)(2,1)S(1)}, u32[]{:S(2)}, u32[]{:S(2)}) collective-permute-start(bf16[24,1536]{1,0:T(8,128)(2,1)} %reduce_sum.12), channel_id=1, source_target_pairs={{0,8},{4,12},{8,0},{12,4},{16,24},{20,28},{24,16},{28,20},{1,9},{5... | collective-permute-start | bytes 221192 | tf_op jit(solution)/shard_map/ppermute | solution.py:347
  79.8 5.7 %collective-permute-start.7 = (bf16[24,1536]{1,0:T(8,128)(2,1)}, bf16[24,1536]{1,0:T(8,128)(2,1)S(1)}, u32[]{:S(2)}, u32[]{:S(2)}) collective-permute-start(bf16[24,1536]{1,0:T(8,128)(2,1)} %reduce_sum.12), channel_id=1, source_target_pairs={{0,4},{4,0},{8,12},{12,8},{16,20},{20,16},{24,28},{28,24},{1,5},{5... | collective-permute-start | bytes 221192 | tf_op jit(solution)/shard_map/ppermute | solution.py:347
  87.3 9.2 %collective-permute-start.12 = (bf16[24,1536]{1,0:T(8,128)(2,1)S(1)}, bf16[24,1536]{1,0:T(8,128)(2,1)S(1)}, u32[]{:S(2)}, u32[]{:S(2)}) collective-permute-start(bf16[24,1536]{1,0:T(8,128)(2,1)S(1)} %add_add_fusion), channel_id=1, source_target_pairs={{0,16},{4,20},{8,24},{12,28},{16,0},{20,4},{24,8},{28,12},{1,17},{... | collective-permute-start | bytes 221192 | tf_op jit(solution)/shard_map/ppermute | solution.py:347
  97.6 30.4 %all-to-all-start.1 = ((bf16[16,24,1536]{2,1,0:T(8,128)(2,1)}), bf16[16,24,1536]{2,1,0:T(8,128)(2,1)S(1)}, u32[]{:S(2)}, u32[]{:S(2)}) async-start(bf16[16,24,1536]{2,1,0:T(8,128)(2,1)} %broadcast_in_dim.19), calls=%async_computation.1 | async-start | bytes 2359296 | tf_op jit(solution)/shard_map/all_to_all | solution.py:364
  103.7 19.6 %collective-permute-start.13 = (bf16[2,96,768]{2,1,0:T(8,128)(2,1)}, bf16[2,96,768]{2,1,0:T(8,128)(2,1)S(1)}, u32[]{:S(2)}, u32[]{:S(2)}) collective-permute-start(bf16[2,96,768]{2,1,0:T(8,128)(2,1)} %get-tuple-element.57), channel_id=1, source_target_pairs={{0,32},{32,64},{64,96},{96,128},{128,160},{160,192},{192,224},{1,3... | collective-permute-start | bytes 884744 | tf_op jit(solution)/shard_map/ppermute | solution.py:338
  106.8 18.3 %collective-permute-start.14 = (bf16[2,96,768]{2,1,0:T(8,128)(2,1)}, bf16[2,96,768]{2,1,0:T(8,128)(2,1)}, u32[]{:S(2)}, u32[]{:S(2)}) collective-permute-start(bf16[2,96,768]{2,1,0:T(8,128)(2,1)} %get-tuple-element.58), channel_id=1, source_target_pairs={{32,0},{64,32},{96,64},{128,96},{160,128},{192,160},{224,192},{33,... | collective-permute-start | bytes 884744 | tf_op jit(solution)/shard_map/ppermute | solution.py:338
  128.0 5.1 %collective-permute-start.15 = (bf16[384,1536]{1,0:T(8,128)(2,1)S(1)}, bf16[384,1536]{1,0:T(8,128)(2,1)S(1)}, u32[]{:S(2)}, u32[]{:S(2)}) collective-permute-start(bf16[384,1536]{1,0:T(8,128)(2,1)S(1)} %bitcast.16), channel_id=1, source_target_pairs={{0,1},{1,0},{2,3},{3,2},{4,5},{5,4},{6,7},{7,6},{8,9},{9,8},{10,11... | collective-permute-start | bytes 3538952 | tf_op jit(solution)/shard_map/ppermute | solution.py:347
  (9 other events, 31.6 us)

commit v4 on v3

--- a/solution.py
+++ b/solution.py
@@ -76,7 +76,7 @@
     key_rows = (first_row + rows)[:, :, None]
     near = jnp.abs(cols[:, :, None] - query_cols[:, None, :]) <= REACH
     keep = (key_rows >= start) & (key_rows < start + WIN) & near
-    return jnp.where(keep, 0.0, -1e30).astype(F32)
+    return jnp.where(keep, 0.0, -1e30).astype(BF16)
 
 
 def sent_cols(core):
@@ -170,7 +170,7 @@
     values = (v_ref[...], *(ref[1] for ref in halo_refs))
     for tile in range(TILES):
         span = slice(tile * TILE_Q, (tile + 1) * TILE_Q)
-        scores = dot(tile_keys(tile, *keys), q_ref[span, :], ((1,), (1,))) * SCALE + bias_ref[tile]
+        scores = dot(tile_keys(tile, *keys), q_ref[span, :], ((1,), (1,))) * SCALE + bias_ref[tile].astype(F32)
         top = jnp.max(scores, axis=0, keepdims=True)
         exponent = jnp.exp(scores - top)
         total = jnp.sum(exponent, axis=0, keepdims=True)
@@ -193,7 +193,7 @@
     for tile in range(TILES):
         span = slice(tile * TILE_Q, (tile + 1) * TILE_Q)
         key_tile = tile_keys(tile, *keys)
-        scores = dot(key_tile, q_ref[span, :], ((1,), (1,))) * SCALE + bias_ref[tile]
+        scores = dot(key_tile, q_ref[span, :], ((1,), (1,))) * SCALE + bias_ref[tile].astype(F32)
         prob = jnp.exp(scores - lse_ref[0, tile : tile + 1, :])
         grad_prob = dot(tile_keys(tile, *values), g_ref[span, :], ((1,), (1,)))
         delta = jnp.sum(prob * grad_prob, axis=0, keepdims=True)

time: 136 us -> 136 us (level)
  no operation moved by 1% of the time
where the time goes in v4:
time: 136 us; the launch traced here: 135 us
  starting transfers between devices  52.4 us (39%)
  waiting for transfers between devices  35.2 us (26%)
  Pallas kernels  32.1 us (24%)
  matrix products  8.05 us (6%)
  other arithmetic  3.53 us (3%)
  local copies, waits for them, and re-layouts  2.62 us (2%)
    ppermute x9, starting transfers between devices, swapped(): lax.ppermute(block, axis, [(i, i ^ bit) for i in range(lax.axis_size(axis...  21.7 us
    ppermute x4, waiting for transfers between devices, along_lat(): lax.ppermute(block, LAT, [(i, i + by) for i in range(bands) if 0 <= i + b...  16.5 us
    ppermute x4, starting transfers between devices, along_lat(): lax.ppermute(block, LAT, [(i, i + by) for i in range(bands) if 0 <= i + b...  14.8 us
    all_to_all x2, starting transfers between devices, plane_sum(): lax.all_to_all(pair.reshape(group, HALF // group, WIDTH), PLANE, split_ax...  12.3 us
    pallas_call x4, Pallas kernels, with_picks(): pl.pallas_call(kernel, grid_spec=pltpu.PrefetchScalarGridSpec(num_scalar_...  10.2 us
    ppermute x3, waiting for transfers between devices, with_next_chip(): lax.ppermute(block, LON, [(j, (j + 2 * (j % 2) - 1) % strips) for j in ra...  9.36 us
    pallas_call x1, Pallas kernels, backward_attention(): pl.pallas_call(backward_kernel, grid_spec=pltpu.PrefetchScalarGridSpec(nu...  9.26 us
    pallas_call x2, Pallas kernels, forward_attention(): pl.pallas_call(forward_kernel, grid_spec=pltpu.PrefetchScalarGridSpec(num...  8.94 us
  transfers between devices with their start and end apart: 18, of which 11 were waited for; matrix products, arithmetic and copies ran while one was open for 5% of the time, Pallas kernels for 17%

profile of v4, /device:TPU:3, one launch (start us, length us, event | category | flops | bytes accessed | tf_op | source)
XLA Modules:
  0.0 134.8 jit_solution(5975263205231621417)
XLA Ops:
  0.7 2.6 %shard_map.165 = (bf16[2,96,768]{2,1,0:T(8,128)(2,1)}, bf16[2,96,768]{2,1,0:T(8,128)(2,1)}, bf16[2,96,768]{2,1,0:T(8,128)(2,1)}, bf16[2,96,768]{2,1,0:T(8,128)(2,1)}) custom-call(s32[1]{0:T(128)} %bitcast.core_ref.which_ref, bf16[2,192,256]{2,1,0:T(8,128)(2,1)} %constant.57.clone.picks_ref, bf16[256,768]{1,0:T(8,128)(2,1)} %bitcast.24, bf16[256,768]{1,0:T(8,128)(2,1)} %bitcast.28), custom_call_target="tpu_custom_call" | custom-call | flops 1000000000 | bytes 2000000 | tf_op jit(solution)/shard_map/pallas_call | solution.py:114
  3.3 3.2 %collective-permute-start = (bf16[2,96,768]{2,1,0:T(8,128)(2,1)}, bf16[2,96,768]{2,1,0:T(8,128)(2,1)S(1)}, u32[]{:S(2)}, u32[]{:S(2)}) collective-permute-start(bf16[2,96,768]{2,1,0:T(8,128)(2,1)} %get-tuple-element.34), channel_id=1, source_target_pairs={{0,32},{32,64},{64,96},{96,128},{128,160},{160,192},{192,224},{1,3... | collective-permute-start | bytes 884744 | tf_op jit(solution)/shard_map/ppermute | solution.py:338
  6.5 4.2 %collective-permute-start.1 = (bf16[2,96,768]{2,1,0:T(8,128)(2,1)}, bf16[2,96,768]{2,1,0:T(8,128)(2,1)S(1)}, u32[]{:S(2)}, u32[]{:S(2)}) collective-permute-start(bf16[2,96,768]{2,1,0:T(8,128)(2,1)} %get-tuple-element.35), channel_id=1, source_target_pairs={{32,0},{64,32},{96,64},{128,96},{160,128},{192,160},{224,192},{33,... | collective-permute-start | bytes 884744 | tf_op jit(solution)/shard_map/ppermute | solution.py:338
  19.2 6.5 %collective-permute-start.4 = (bf16[2,80,768]{2,1,0:T(8,128)(2,1)}, bf16[2,80,768]{2,1,0:T(8,128)(2,1)S(1)}, u32[]{:S(2)}, u32[]{:S(2)}) collective-permute-start(bf16[2,80,768]{2,1,0:T(8,128)(2,1)} %get-tuple-element.38), channel_id=1, source_target_pairs={{0,1},{1,0},{2,3},{3,2},{4,5},{5,4},{6,7},{7,6},{8,9},{9,8},{10,11... | collective-permute-start | bytes 737288 | tf_op jit(solution)/shard_map/ppermute | solution.py:347
  27.0 8.6 %collective-permute-done.5.refs_5_ = bf16[2,80,768]{2,1,0:T(8,128)(2,1)S(1)} collective-permute-done((bf16[2,80,768]{2,1,0:T(8,128)(2,1)}, bf16[2,80,768]{2,1,0:T(8,128)(2,1)S(1)}, u32[]{:S(2)}, u32[]{:S(2)}) %collective-permute-start.5) | collective-permute-done | bytes 245792 | tf_op jit(solution)/shard_map/ppermute | solution.py:343
  36.4 4.5 %shard_map.168 = (bf16[256,384]{1,0:T(8,128)(2,1)}, f32[3,8,128]{2,1,0:T(8,128)}) custom-call(s32[1]{0:T(128)S(6)} %mul.16.base_ref.shift_ref, bf16[256,768]{1,0:T(8,128)(2,1)} %bitcast.21, bf16[256,768]{1,0:T(8,128)(2,1)} %bitcast.25, bf16[256,768]{1,0:T(8,128)(2,1)} %bitcast.29, bf16[2,96,768]{2,1,0:T(8,128)(2,1)} %copy-done.9, ...), custom_call_target="tpu_custom_call" | custom-call | flops 2000000000 | bytes 6000000 | tf_op jit(solution)/shard_map/pallas_call | solution.py:235
  40.9 2.4 %convolution_convert_fusion = bf16[384,1536]{1,0:T(8,128)(2,1)} fusion(bf16[256,384]{1,0:T(8,128)(2,1)} %get-tuple-element.41, bf16[256,1536]{1,0:T(8,128)(2,1)S(1)} %bitcast.19), kind=kOutput, calls=%fused_computation.2 | convolution fusion | flops 302579712 | bytes 2162688 | tf_op jit(solution)/shard_map/dot_general | solution.py:108
  43.6 4.4 %shard_map.167 = (bf16[256,384]{1,0:T(8,128)(2,1)}, f32[3,8,128]{2,1,0:T(8,128)}) custom-call(s32[1]{0:T(128)S(6)} %mul.13.base_ref, bf16[256,768]{1,0:T(8,128)(2,1)} %bitcast.22, bf16[256,768]{1,0:T(8,128)(2,1)} %bitcast.26, bf16[256,768]{1,0:T(8,128)(2,1)} %bitcast.30, bf16[2,96,768]{2,1,0:T(8,128)(2,1)} %copy-done.9, bf16[2,96,768]{2,1,0:T(8,128)(2,1)} %copy-done.10, ...), custom_call_target="tpu_custom_call" | custom-call | flops 2000000000 | bytes 6000000 | tf_op jit(solution)/shard_map/pallas_call | solution.py:235
  48.1 2.9 %fusion = bf16[384,1536]{1,0:T(8,128)(2,1)} fusion(bf16[256,384]{1,0:T(8,128)(2,1)} %get-tuple-element.40, bf16[256,1536]{1,0:T(8,128)(2,1)S(1)} %bitcast.20, bf16[384,1536]{1,0:T(8,128)(2,1)} %collective-permute-done.6), kind=kOutput, calls=%fused_computation.1 | convolution fusion | flops 303759360 | bytes 3342336 | tf_op jit(solution)/shard_map/dot_general | solution.py:108
  51.0 6.3 %all-to-all-start = ((bf16[16,24,1536]{2,1,0:T(8,128)(2,1)}), bf16[16,24,1536]{2,1,0:T(8,128)(2,1)S(1)}, u32[]{:S(2)}, u32[]{:S(2)}) async-start(bf16[16,24,1536]{2,1,0:T(8,128)(2,1)} %bitcast.5), calls=%async_computation | async-start | bytes 2359296 | tf_op jit(solution)/shard_map/all_to_all | solution.py:364
  57.3 2.7 %convolution_convert_fusion.1.refs_7_ = bf16[256,768]{1,0:T(8,128)(2,1)} fusion(bf16[256,1536]{1,0:T(8,128)(2,1)} %bitcast.18, bf16[768,1536]{1,0:T(8,128)(2,1)S(1)} %copy-done), kind=kOutput, calls=%fused_computation.3 | convolution fusion | flops 604176384 | bytes 3538944 | tf_op jit(solution)/shard_map/dot_general | solution.py:108
  60.6 9.3 %shard_map.169 = (bf16[256,768]{1,0:T(8,128)(2,1)}, f32[2,256,768]{2,1,0:T(8,128)}, f32[2,192,768]{2,1,0:T(8,128)}, bf16[2,176,768]{2,1,0:T(8,128)(2,1)}, bf16[2,176,768]{2,1,0:T(8,128)(2,1)}) custom-call(s32[1]{0:T(128)S(6)} %mul.16.base_ref.shift_ref, bf16[256,768]{1,0:T(8,128)(2,1)} %bitcast.23, bf16[256,768]{1,0:T(8,128)(2,1)} %bitcast.27, ...), custom_call_target="tpu_custom_call" | custom-call | flops 6000000000 | bytes 12000000 | tf_op jit(solution)/shard_map/pallas_call | solution.py:255
  72.3 3.2 %all-to-all-done = bf16[16,24,1536]{2,1,0:T(8,128)(2,1)S(1)} async-done(((bf16[16,24,1536]{2,1,0:T(8,128)(2,1)}), bf16[16,24,1536]{2,1,0:T(8,128)(2,1)S(1)}, u32[]{:S(2)}, u32[]{:S(2)}) %all-to-all-start) | async-done | bytes 1179680 | tf_op jit(solution)/shard_map/all_to_all | solution.py:364
  76.3 3.4 %collective-permute-start.9 = (bf16[24,1536]{1,0:T(8,128)(2,1)}, bf16[24,1536]{1,0:T(8,128)(2,1)S(1)}, u32[]{:S(2)}, u32[]{:S(2)}) collective-permute-start(bf16[24,1536]{1,0:T(8,128)(2,1)} %reduce_sum.12), channel_id=1, source_target_pairs={{0,12},{4,8},{8,4},{12,0},{16,28},{20,24},{24,20},{28,16},{1,13},{... | collective-permute-start | bytes 221192 | tf_op jit(solution)/shard_map/ppermute | solution.py:347
  80.0 2.9 %collective-permute-done.9 = bf16[24,1536]{1,0:T(8,128)(2,1)S(1)} collective-permute-done((bf16[24,1536]{1,0:T(8,128)(2,1)}, bf16[24,1536]{1,0:T(8,128)(2,1)S(1)}, u32[]{:S(2)}, u32[]{:S(2)}) %collective-permute-start.9) | collective-permute-done | bytes 73760 | tf_op jit(solution)/shard_map/ppermute | solution.py:347
  82.9 2.5 %collective-permute-done.8 = bf16[24,1536]{1,0:T(8,128)(2,1)S(1)} collective-permute-done((bf16[24,1536]{1,0:T(8,128)(2,1)}, bf16[24,1536]{1,0:T(8,128)(2,1)S(1)}, u32[]{:S(2)}, u32[]{:S(2)}) %collective-permute-start.8) | collective-permute-done | bytes 73760 | tf_op jit(solution)/shard_map/ppermute | solution.py:347
  87.1 6.6 %collective-permute-start.12 = (bf16[24,1536]{1,0:T(8,128)(2,1)S(1)}, bf16[24,1536]{1,0:T(8,128)(2,1)S(1)}, u32[]{:S(2)}, u32[]{:S(2)}) collective-permute-start(bf16[24,1536]{1,0:T(8,128)(2,1)S(1)} %add_add_fusion), channel_id=1, source_target_pairs={{0,16},{4,20},{8,24},{12,28},{16,0},{20,4},{24,8},{28,12},{1,17},{... | collective-permute-start | bytes 221192 | tf_op jit(solution)/shard_map/ppermute | solution.py:347
  93.7 2.5 %shard_map.170 = (bf16[2,96,768]{2,1,0:T(8,128)(2,1)}, bf16[2,96,768]{2,1,0:T(8,128)(2,1)}) custom-call(s32[1]{0:T(128)} %bitcast.core_ref.which_ref, bf16[2,192,160]{2,1,0:T(8,128)(2,1)} %constant.64.clone.spread_ref, f32[2,192,768]{2,1,0:T(8,128)} %get-tuple-element.50.poles_ref, bf16[2,176,768]{2,1,0:T(8,128)(2,1)} %collective-permute-done.10.chip_ref, ...), custom_call_target="tpu_custom_call" | custom-call | flops 1000000000 | bytes 4000000 | tf_op jit(solution)/shard_map/pallas_call | solution.py:114
  97.4 6.1 %all-to-all-start.1 = ((bf16[16,24,1536]{2,1,0:T(8,128)(2,1)}), bf16[16,24,1536]{2,1,0:T(8,128)(2,1)S(1)}, u32[]{:S(2)}, u32[]{:S(2)}) async-start(bf16[16,24,1536]{2,1,0:T(8,128)(2,1)} %broadcast_in_dim.19), calls=%async_computation.1 | async-start | bytes 2359296 | tf_op jit(solution)/shard_map/all_to_all | solution.py:364
  103.5 3.1 %collective-permute-start.13 = (bf16[2,96,768]{2,1,0:T(8,128)(2,1)}, bf16[2,96,768]{2,1,0:T(8,128)(2,1)S(1)}, u32[]{:S(2)}, u32[]{:S(2)}) collective-permute-start(bf16[2,96,768]{2,1,0:T(8,128)(2,1)} %get-tuple-element.57), channel_id=1, source_target_pairs={{0,32},{32,64},{64,96},{96,128},{128,160},{160,192},{192,224},{1,3... | collective-permute-start | bytes 884744 | tf_op jit(solution)/shard_map/ppermute | solution.py:338
  106.6 4.3 %collective-permute-start.14 = (bf16[2,96,768]{2,1,0:T(8,128)(2,1)}, bf16[2,96,768]{2,1,0:T(8,128)(2,1)}, u32[]{:S(2)}, u32[]{:S(2)}) collective-permute-start(bf16[2,96,768]{2,1,0:T(8,128)(2,1)} %get-tuple-element.58), channel_id=1, source_target_pairs={{32,0},{64,32},{96,64},{128,96},{160,128},{192,160},{224,192},{33,... | collective-permute-start | bytes 884744 | tf_op jit(solution)/shard_map/ppermute | solution.py:338
  110.9 12.2 %collective-permute-done.13.from_north_ref = bf16[2,96,768]{2,1,0:T(8,128)(2,1)S(1)} collective-permute-done((bf16[2,96,768]{2,1,0:T(8,128)(2,1)}, bf16[2,96,768]{2,1,0:T(8,128)(2,1)S(1)}, u32[]{:S(2)}, u32[]{:S(2)}) %collective-permute-start.13) | collective-permute-done | bytes 294944 | tf_op jit(solution)/shard_map/ppermute | solution.py:338
  124.9 2.9 %shard_map.171 = (bf16[256,768]{1,0:T(8,128)(2,1)}, bf16[256,768]{1,0:T(8,128)(2,1)}) custom-call(s32[1]{0:T(128)} %bitcast.core_ref.which_ref, bf16[2,256,192]{2,1,0:T(8,128)(2,1)} %constant.65.clone.spread_ref, f32[2,256,768]{2,1,0:T(8,128)} %get-tuple-element.56.own_ref, bf16[2,176,768]{2,1,0:T(8,128)(2,1)} %collective-permute-done.10.chip_ref, ...), custom_call_target="tpu_custom_call" | custom-call | flops 1000000000 | bytes 6000000 | tf_op jit(solution)/shard_map/pallas_call | solution.py:114
  127.8 2.7 %collective-permute-start.15 = (bf16[384,1536]{1,0:T(8,128)(2,1)S(1)}, bf16[384,1536]{1,0:T(8,128)(2,1)S(1)}, u32[]{:S(2)}, u32[]{:S(2)}) collective-permute-start(bf16[384,1536]{1,0:T(8,128)(2,1)S(1)} %bitcast.16), channel_id=1, source_target_pairs={{0,1},{1,0},{2,3},{3,2},{4,5},{5,4},{6,7},{7,6},{8,9},{9,8},{10,11... | collective-permute-start | bytes 3538952 | tf_op jit(solution)/shard_map/ppermute | solution.py:347
  (62 shorter events, 23.9 us)
Async XLA Ops:
  0.6 56.6 %copy-start = (bf16[768,1536]{1,0:T(8,128)(2,1)S(1)}, bf16[768,1536]{1,0:T(8,128)(2,1)}, u32[]{:S(2)}) copy-start(bf16[768,1536]{1,0:T(8,128)(2,1)} %param.18) | copy-start | bytes 7077892
  0.7 13.2 %copy-start.4 = (s32[2,608]{1,0:T(2,128)S(1)}, s32[2,608]{1,0:T(2,128)}, u32[]{:S(2)}) copy-start(s32[2,608]{1,0:T(2,128)} %constant.62.clone) | copy-start | bytes 14596
  0.7 13.2 %copy-start.5 = (s32[2,608]{1,0:T(2,128)S(1)}, s32[2,608]{1,0:T(2,128)}, u32[]{:S(2)}) copy-start(s32[2,608]{1,0:T(2,128)} %constant.60.clone) | copy-start | bytes 14596
  0.7 13.2 %copy-start.6 = (s32[2,608]{1,0:T(2,128)S(1)}, s32[2,608]{1,0:T(2,128)}, u32[]{:S(2)}) copy-start(s32[2,608]{1,0:T(2,128)} %constant.59.clone) | copy-start | bytes 14596
  3.3 12.1 %collective-permute-start = (bf16[2,96,768]{2,1,0:T(8,128)(2,1)}, bf16[2,96,768]{2,1,0:T(8,128)(2,1)S(1)}, u32[]{:S(2)}, u32[]{:S(2)}) collective-permute-start(bf16[2,96,768]{2,1,0:T(8,128)(2,1)} %get-tuple-element.34), channel_id=1, source_target_pairs={{0,32},{32,64},{64,96},{96,128},{128,160},{160,192},{192,224},{1,3... | collective-permute-start | bytes 884744 | tf_op jit(solution)/shard_map/ppermute | solution.py:338
  6.5 9.9 %collective-permute-start.1 = (bf16[2,96,768]{2,1,0:T(8,128)(2,1)}, bf16[2,96,768]{2,1,0:T(8,128)(2,1)S(1)}, u32[]{:S(2)}, u32[]{:S(2)}) collective-permute-start(bf16[2,96,768]{2,1,0:T(8,128)(2,1)} %get-tuple-element.35), channel_id=1, source_target_pairs={{32,0},{64,32},{96,64},{128,96},{160,128},{192,160},{224,192},{33,... | collective-permute-start | bytes 884744 | tf_op jit(solution)/shard_map/ppermute | solution.py:338
  10.7 16.2 %collective-permute-start.2 = (bf16[2,96,768]{2,1,0:T(8,128)(2,1)}, bf16[2,96,768]{2,1,0:T(8,128)(2,1)S(1)}, u32[]{:S(2)}, u32[]{:S(2)}) collective-permute-start(bf16[2,96,768]{2,1,0:T(8,128)(2,1)} %get-tuple-element.36), channel_id=1, source_target_pairs={{0,1},{1,0},{2,3},{3,2},{4,5},{5,4},{6,7},{7,6},{8,9},{9,8},{10,11... | collective-permute-start | bytes 884744 | tf_op jit(solution)/shard_map/ppermute | solution.py:347
  12.0 14.9 %collective-permute-start.3 = (bf16[2,96,768]{2,1,0:T(8,128)(2,1)}, bf16[2,96,768]{2,1,0:T(8,128)(2,1)}, u32[]{:S(2)}, u32[]{:S(2)}) collective-permute-start(bf16[2,96,768]{2,1,0:T(8,128)(2,1)} %get-tuple-element.37), channel_id=1, source_target_pairs={{0,31},{1,2},{2,1},{3,4},{4,3},{5,6},{6,5},{7,8},{8,7},{9,10},{10,... | collective-permute-start | bytes 884744 | tf_op jit(solution)/shard_map/ppermute | solution.py:343
  13.8 11.8 %copy-start.8 = (s32[2,128]{1,0:T(2,128)S(1)}, s32[2,128]{1,0:T(2,128)}, u32[]{:S(2)}) copy-start(s32[2,128]{1,0:T(2,128)} %constant.61.clone) | copy-start | bytes 3076
  13.9 11.8 %copy-start.7 = (s32[2,128]{1,0:T(2,128)S(1)}, s32[2,128]{1,0:T(2,128)}, u32[]{:S(2)}) copy-start(s32[2,128]{1,0:T(2,128)} %constant.71) | copy-start | bytes 3076
  19.2 7.8 %collective-permute-start.4 = (bf16[2,80,768]{2,1,0:T(8,128)(2,1)}, bf16[2,80,768]{2,1,0:T(8,128)(2,1)S(1)}, u32[]{:S(2)}, u32[]{:S(2)}) collective-permute-start(bf16[2,80,768]{2,1,0:T(8,128)(2,1)} %get-tuple-element.38), channel_id=1, source_target_pairs={{0,1},{1,0},{2,3},{3,2},{4,5},{5,4},{6,7},{7,6},{8,9},{9,8},{10,11... | collective-permute-start | bytes 737288 | tf_op jit(solution)/shard_map/ppermute | solution.py:347
  25.7 10.0 %collective-permute-start.5 = (bf16[2,80,768]{2,1,0:T(8,128)(2,1)}, bf16[2,80,768]{2,1,0:T(8,128)(2,1)S(1)}, u32[]{:S(2)}, u32[]{:S(2)}) collective-permute-start(bf16[2,80,768]{2,1,0:T(8,128)(2,1)} %get-tuple-element.39), channel_id=1, source_target_pairs={{0,31},{1,2},{2,1},{3,4},{4,3},{5,6},{6,5},{7,8},{8,7},{9,10},{10,... | collective-permute-start | bytes 737288 | tf_op jit(solution)/shard_map/ppermute | solution.py:343
  43.3 4.7 %collective-permute-start.6 = (bf16[384,1536]{1,0:T(8,128)(2,1)}, bf16[384,1536]{1,0:T(8,128)(2,1)}, u32[]{:S(2)}, u32[]{:S(2)}) collective-permute-start(bf16[384,1536]{1,0:T(8,128)(2,1)} %convolution_convert_fusion), channel_id=1, source_target_pairs={{0,1},{1,0},{2,3},{3,2},{4,5},{5,4},{6,7},{7,6},{8,9},{9,8},{10,11... | collective-permute-start | bytes 3538952 | tf_op jit(solution)/shard_map/ppermute | solution.py:347
  51.0 24.5 %all-to-all-start = ((bf16[16,24,1536]{2,1,0:T(8,128)(2,1)}), bf16[16,24,1536]{2,1,0:T(8,128)(2,1)S(1)}, u32[]{:S(2)}, u32[]{:S(2)}) async-start(bf16[16,24,1536]{2,1,0:T(8,128)(2,1)} %bitcast.5), calls=%async_computation | async-start | bytes 2359296 | tf_op jit(solution)/shard_map/all_to_all | solution.py:364
  69.9 16.5 %collective-permute-start.10 = (bf16[2,176,768]{2,1,0:T(8,128)(2,1)}, bf16[2,176,768]{2,1,0:T(8,128)(2,1)}, u32[]{:S(2)}, u32[]{:S(2)}) collective-permute-start(bf16[2,176,768]{2,1,0:T(8,128)(2,1)} %get-tuple-element.47), channel_id=1, source_target_pairs={{0,1},{1,0},{2,3},{3,2},{4,5},{5,4},{6,7},{7,6},{8,9},{9,8},{10,11... | collective-permute-start | bytes 1622024 | tf_op jit(solution)/shard_map/ppermute | solution.py:347
  70.5 16.6 %collective-permute-start.11 = (bf16[2,176,768]{2,1,0:T(8,128)(2,1)}, bf16[2,176,768]{2,1,0:T(8,128)(2,1)}, u32[]{:S(2)}, u32[]{:S(2)}) collective-permute-start(bf16[2,176,768]{2,1,0:T(8,128)(2,1)} %get-tuple-element.48), channel_id=1, source_target_pairs={{0,31},{1,2},{2,1},{3,4},{4,3},{5,6},{6,5},{7,8},{8,7},{9,10},{10,... | collective-permute-start | bytes 1622024 | tf_op jit(solution)/shard_map/ppermute | solution.py:343
  76.3 6.6 %collective-permute-start.9 = (bf16[24,1536]{1,0:T(8,128)(2,1)}, bf16[24,1536]{1,0:T(8,128)(2,1)S(1)}, u32[]{:S(2)}, u32[]{:S(2)}) collective-permute-start(bf16[24,1536]{1,0:T(8,128)(2,1)} %reduce_sum.12), channel_id=1, source_target_pairs={{0,12},{4,8},{8,4},{12,0},{16,28},{20,24},{24,20},{28,16},{1,13},{... | collective-permute-start | bytes 221192 | tf_op jit(solution)/shard_map/ppermute | solution.py:347
  79.7 5.7 %collective-permute-start.8 = (bf16[24,1536]{1,0:T(8,128)(2,1)}, bf16[24,1536]{1,0:T(8,128)(2,1)S(1)}, u32[]{:S(2)}, u32[]{:S(2)}) collective-permute-start(bf16[24,1536]{1,0:T(8,128)(2,1)} %reduce_sum.12), channel_id=1, source_target_pairs={{0,8},{4,12},{8,0},{12,4},{16,24},{20,28},{24,16},{28,20},{1,9},{5... | collective-permute-start | bytes 221192 | tf_op jit(solution)/shard_map/ppermute | solution.py:347
  79.7 5.7 %collective-permute-start.7 = (bf16[24,1536]{1,0:T(8,128)(2,1)}, bf16[24,1536]{1,0:T(8,128)(2,1)S(1)}, u32[]{:S(2)}, u32[]{:S(2)}) collective-permute-start(bf16[24,1536]{1,0:T(8,128)(2,1)} %reduce_sum.12), channel_id=1, source_target_pairs={{0,4},{4,0},{8,12},{12,8},{16,20},{20,16},{24,28},{28,24},{1,5},{5... | collective-permute-start | bytes 221192 | tf_op jit(solution)/shard_map/ppermute | solution.py:347
  87.1 9.2 %collective-permute-start.12 = (bf16[24,1536]{1,0:T(8,128)(2,1)S(1)}, bf16[24,1536]{1,0:T(8,128)(2,1)S(1)}, u32[]{:S(2)}, u32[]{:S(2)}) collective-permute-start(bf16[24,1536]{1,0:T(8,128)(2,1)S(1)} %add_add_fusion), channel_id=1, source_target_pairs={{0,16},{4,20},{8,24},{12,28},{16,0},{20,4},{24,8},{28,12},{1,17},{... | collective-permute-start | bytes 221192 | tf_op jit(solution)/shard_map/ppermute | solution.py:347
  97.4 30.4 %all-to-all-start.1 = ((bf16[16,24,1536]{2,1,0:T(8,128)(2,1)}), bf16[16,24,1536]{2,1,0:T(8,128)(2,1)S(1)}, u32[]{:S(2)}, u32[]{:S(2)}) async-start(bf16[16,24,1536]{2,1,0:T(8,128)(2,1)} %broadcast_in_dim.19), calls=%async_computation.1 | async-start | bytes 2359296 | tf_op jit(solution)/shard_map/all_to_all | solution.py:364
  103.5 19.6 %collective-permute-start.13 = (bf16[2,96,768]{2,1,0:T(8,128)(2,1)}, bf16[2,96,768]{2,1,0:T(8,128)(2,1)S(1)}, u32[]{:S(2)}, u32[]{:S(2)}) collective-permute-start(bf16[2,96,768]{2,1,0:T(8,128)(2,1)} %get-tuple-element.57), channel_id=1, source_target_pairs={{0,32},{32,64},{64,96},{96,128},{128,160},{160,192},{192,224},{1,3... | collective-permute-start | bytes 884744 | tf_op jit(solution)/shard_map/ppermute | solution.py:338
  106.6 18.3 %collective-permute-start.14 = (bf16[2,96,768]{2,1,0:T(8,128)(2,1)}, bf16[2,96,768]{2,1,0:T(8,128)(2,1)}, u32[]{:S(2)}, u32[]{:S(2)}) collective-permute-start(bf16[2,96,768]{2,1,0:T(8,128)(2,1)} %get-tuple-element.58), channel_id=1, source_target_pairs={{32,0},{64,32},{96,64},{128,96},{160,128},{192,160},{224,192},{33,... | collective-permute-start | bytes 884744 | tf_op jit(solution)/shard_map/ppermute | solution.py:338
  127.8 5.2 %collective-permute-start.15 = (bf16[384,1536]{1,0:T(8,128)(2,1)S(1)}, bf16[384,1536]{1,0:T(8,128)(2,1)S(1)}, u32[]{:S(2)}, u32[]{:S(2)}) collective-permute-start(bf16[384,1536]{1,0:T(8,128)(2,1)S(1)} %bitcast.16), channel_id=1, source_target_pairs={{0,1},{1,0},{2,3},{3,2},{4,5},{5,4},{6,7},{7,6},{8,9},{9,8},{10,11... | collective-permute-start | bytes 3538952 | tf_op jit(solution)/shard_map/ppermute | solution.py:347
  (9 other events, 31.6 us)
